TPU v7x, 128 devices: a whole 4x4x4 slice. The times are simulated.
128 devices in a mesh: pool: 2 (over core), grp: 8 (over x, z_lo), shard: 8 (over y, z_hi).
Axes of the slice: x: 4, y: 4, z: 4 (z_hi: 2, z_lo: 2; z = z_hi * 2 + z_lo), core: 2. Of those that a mesh axis runs over, the one named last changes fastest.
Arguments:
- queries: bfloat16 [1024, 6144], P(('grp', 'shard'), 'pool')
- new_keys: bfloat16 [1024, 1024], P(('grp', 'shard'), 'pool'), may hold values from -6 to 6
- new_values: bfloat16 [1024, 1024], P(('grp', 'shard'), 'pool'), may hold values from -6 to 6
- fork_map: int32 [1024], P(('grp', 'shard')), may hold values from 0 to 127, as said below
- key_cache: bfloat16 [128, 1024, 1024], P(('grp', 'shard'), None, 'pool')
- value_cache: bfloat16 [128, 1024, 1024], P(('grp', 'shard'), None, 'pool'), may hold values from -6 to 6
- cache_lengths: int32 [128], P(('grp', 'shard')), may hold values from 256 to 1024
- residual: bfloat16 [1024, 6144], P(('grp', 'shard')), may hold values from -1.75 to 1.75
- norm_gain: bfloat16 [6144], replicated, may hold values from 0.5 to 1.5
- expert_ids: int32 [1024, 2], P(('grp', 'shard')), may hold values from 0 to 7, all different within a row; in each aligned block of 16 rows (0 to 15, 16 to 31, ...) at most 8 rows name the same one
- gate_weights: float32 [1024, 2], P(('grp', 'shard')), may hold values from 0.1 to 1
- w_gate: bfloat16 [8, 6144, 8192], P('grp', None, ('pool', 'shard')), may hold values from -0.078125 to 0.078125
- w_up: bfloat16 [8, 6144, 8192], P('grp', None, ('pool', 'shard')), may hold values from -0.078125 to 0.078125
- w_down: bfloat16 [8, 8192, 6144], P('grp', ('pool', 'shard')), may hold values from -0.0625 to 0.0625
Outputs:
- layer_out: bfloat16 [1024, 6144], P(('grp', 'shard'))
Inputs may be any that keep to these rules, and one draw needn't show every extreme that they name: Row r forks a prompt held beside it: fork_map[r] // 2 == r // 16. `expert_ids`: each row names 2 different experts; among the 16 rows of one device no expert is named more than 8 times.
All inputs are finite; a program needn't handle non-finite values.
Results may differ from a plain program's by a relative error of at most 0.02.
Values may be sent and summed in bfloat16 or wider, within the bound.
A program may use at most 128 MiB of HBM per device.

v0:
```python
import jax
import jax.numpy as jnp
from jax import lax
from jax.sharding import PartitionSpec as P

HD = 128
TOP = 2
CAP = 8


def on_device(
    queries,
    new_keys,
    new_values,
    fork_map,
    key_cache,
    value_cache,
    cache_lengths,
    residual,
    norm_gain,
    expert_ids,
    gate_weights,
    w_gate,
    w_up,
    w_down,
):
    highest = lax.Precision.HIGHEST
    row_count = queries.shape[0]
    kv_local = key_cache.shape[2] // HD
    group = queries.shape[1] // (HD * kv_local)
    prompts_here = key_cache.shape[0]
    cache_len = key_cache.shape[1]
    scale = HD ** (-0.5)
    query_four = queries.reshape(row_count, kv_local, group, HD)
    query_heads = query_four.transpose(1, 0, 2, 3).reshape(kv_local, row_count * group, HD)
    keys = key_cache.reshape(prompts_here * cache_len, kv_local, HD)
    values = value_cache.reshape(prompts_here * cache_len, kv_local, HD)
    scores = (
        jnp.einsum("hqd,thd->hqt", query_heads, keys, preferred_element_type=jnp.float32) * scale
    )
    key_index = jnp.arange(prompts_here * cache_len, dtype=jnp.int32)
    key_prompt = key_index // cache_len
    prompt_match = key_prompt[:, None] == jnp.arange(prompts_here, dtype=jnp.int32)[None, :]
    key_limit = jnp.sum(jnp.where(prompt_match, cache_lengths[None, :], 0), axis=1)
    key_live = key_index % cache_len < key_limit
    row_prompt = jnp.repeat(fork_map % prompts_here, group)
    valid = (row_prompt[:, None] == key_prompt[None, :]) & key_live[None, :]
    own_score = jnp.einsum(
        "rhgd,rhd->hrg",
        query_four,
        new_keys.reshape(row_count, kv_local, HD),
        preferred_element_type=jnp.float32,
    )
    own_score = own_score.reshape(kv_local, row_count * group) * scale
    masked = jnp.where(valid[None], scores, -1e30)
    top = jnp.maximum(jnp.max(masked, axis=-1), own_score)
    raw = jnp.where(valid[None], jnp.exp(masked - top[..., None]), 0.0)
    own_weight = jnp.exp(own_score - top)
    total = jnp.sum(raw, axis=-1) + own_weight
    fresh = new_values.reshape(row_count, kv_local, 1, HD).astype(jnp.float32)
    fresh = (
        jnp.broadcast_to(fresh, (row_count, kv_local, group, HD))
        .transpose(1, 0, 2, 3)
        .reshape(kv_local, row_count * group, HD)
    )
    mixed = jnp.einsum(
        "hqt,thd->hqd", raw.astype(jnp.bfloat16), values, preferred_element_type=jnp.float32
    )
    mixed = mixed + own_weight[..., None] * fresh
    attended = (
        (mixed / total[..., None]).reshape(kv_local, row_count, group, HD).transpose(1, 0, 2, 3)
    )
    attended = attended.reshape(row_count, kv_local * group * HD).astype(jnp.bfloat16)
    attended = lax.all_gather(attended, "pool", axis=1, tiled=True)
    hidden_state = residual.astype(jnp.float32) + attended.astype(jnp.float32)
    meansq = jnp.mean(hidden_state * hidden_state, axis=-1, keepdims=True)
    normed = (hidden_state * lax.rsqrt(meansq + 1e-05) * norm_gain.astype(jnp.float32)).astype(
        jnp.bfloat16
    )
    model_width = normed.shape[1]
    expert_count = lax.axis_size("grp") * w_gate.shape[0]
    chosen = expert_ids.reshape(-1)
    picks = chosen.shape[0]
    expert_axis = jnp.arange(expert_count, dtype=jnp.int32)
    onehot = (chosen[:, None] == expert_axis[None, :]).astype(jnp.int32)
    ranks = jnp.sum((jnp.cumsum(onehot, axis=0) - 1) * onehot, axis=1)
    slot_match = (chosen[None, None, :] == expert_axis[:, None, None]) & (
        ranks[None, None, :] == jnp.arange(CAP, dtype=jnp.int32)[None, :, None]
    )
    slot_match = slot_match.astype(jnp.float32).reshape(expert_count * CAP, picks)
    pick_rows = (
        (jnp.arange(picks, dtype=jnp.int32) // TOP)[:, None]
        == jnp.arange(row_count, dtype=jnp.int32)[None, :]
    ).astype(jnp.float32)
    placing = jnp.dot(slot_match, pick_rows, precision=highest)
    weighting = jnp.dot(
        pick_rows.T, (slot_match * gate_weights.reshape(-1)[None, :]).T, precision=highest
    )
    outgoing = jnp.dot(placing.astype(jnp.bfloat16), normed, preferred_element_type=jnp.float32)
    outgoing = outgoing.astype(jnp.bfloat16).reshape(expert_count, CAP, model_width)
    arrived = lax.all_to_all(outgoing, "grp", split_axis=0, concat_axis=0, tiled=True)
    rows_in = lax.all_gather(arrived[None], "shard", axis=0, tiled=True)
    flat = rows_in.reshape(-1, model_width)
    gate_part = jnp.dot(flat, w_gate[0], preferred_element_type=jnp.float32)
    up_part = jnp.dot(flat, w_up[0], preferred_element_type=jnp.float32)
    inner = (jax.nn.silu(gate_part) * up_part).astype(jnp.bfloat16)
    partial_out = jnp.dot(inner, w_down[0], preferred_element_type=jnp.float32).reshape(
        rows_in.shape
    )
    summed = lax.psum(partial_out.astype(jnp.bfloat16), ("pool", "shard")).astype(jnp.float32)
    owned = lax.dynamic_index_in_dim(summed, lax.axis_index("shard"), 0, keepdims=False)
    returned = lax.all_to_all(
        owned.astype(jnp.bfloat16), "grp", split_axis=0, concat_axis=0, tiled=True
    )
    returned = returned.reshape(expert_count * CAP, model_width).astype(jnp.float32)
    gathered = jnp.dot(weighting, returned, precision=highest)
    return (hidden_state + gathered).astype(jnp.bfloat16)


def solution(mesh):
    in_specs = (
        P(("grp", "shard"), "pool"),
        P(("grp", "shard"), "pool"),
        P(("grp", "shard"), "pool"),
        P(("grp", "shard")),
        P(("grp", "shard"), None, "pool"),
        P(("grp", "shard"), None, "pool"),
        P(("grp", "shard")),
        P(("grp", "shard"), None),
        P(),
        P(("grp", "shard"), None),
        P(("grp", "shard"), None),
        P("grp", None, ("pool", "shard")),
        P("grp", None, ("pool", "shard")),
        P("grp", ("pool", "shard"), None),
    )
    out_specs = P(("grp", "shard"), None)
    return jax.shard_map(
        on_device, mesh=mesh, in_specs=in_specs, out_specs=out_specs, check_vma=False
    )
```

profile of v0, /device:TPU:1, one launch (start us, length us, event | category | flops | bytes accessed | tf_op | source)
XLA Modules:
  0.0 467.3 jit_solution(7371544769927107033)
XLA Ops:
  6.5 0.6 and_select_fusion
  7.1 0.7 fusion.57
  7.9 0.7 and_select_fusion.1
  8.7 1.0 reshape.232
  9.8 4.0 reshape.234
  14.3 2.7 fusion.81
  17.0 0.8 fusion.9
  17.7 0.6 fusion.80
  18.4 3.9 reshape.236
  22.4 2.6 fusion.38
  25.2 3.0 all_gather.6
  28.4 0.8 copy.47
  29.6 0.9 convolution_convert_fusion.2
  30.5 0.4 fusion
  31.0 16.8 %all_to_all.10 = bf16[8,8,6144]{2,1,0:T(8,128)(2,1)} all-to-all(bf16[8,8,6144]{2,1,0:T(8,128)(2,1)S(1)} %fusion), channel_id=1, replica_groups=mesh['pool'=2,'grp'=8,'shard'=8] {'grp'}, dimensions={0} | all-to-all | bytes 1572864 | tf_op jit(solution)/shard_map/all_to_all | solution.py:101
  47.8 91.2 %all-gather.3.cloned.1.call-done = bf16[64,8,6144]{2,1,0:T(8,128)(2,1)} async-done(((bf16[8,8,6144]{2,1,0:T(8,128)(2,1)}), bf16[64,8,6144]{2,1,0:T(8,128)(2,1)}) %all-gather.3.cloned.1.call-update) | async-done | bytes 6291472 | tf_op jit(solution)/shard_map/all_gather | solution.py:102
  139.0 8.1 %fusion.5 = f32[512,512]{1,0:T(8,128)S(1)} fusion(bf16[1,6144,512]{2,1,0:T(8,128)(2,1)} %param.25, bf16[64,8,6144]{2,1,0:T(8,128)(2,1)} %all-gather.3.cloned.1.call-done), kind=kOutput, calls=%fused_computation.8 | convolution fusion | flops 3221225472 | bytes 13631488 | tf_op jit(solution)/shard_map/dot_general | solution.py:104
  147.1 6.4 %fusion.23 = bf16[512,512]{1,0:T(8,128)(2,1)S(1)} fusion(bf16[1,6144,512]{2,1,0:T(8,128)(2,1)} %param.26, bf16[64,8,6144]{2,1,0:T(8,128)(2,1)S(1)} %copy-done.5, f32[512,512]{1,0:T(8,128)S(1)} %fusion.5), kind=kOutput, calls=%fused_computation.24 | convolution fusion | flops 3222798336 | bytes 14155776 | tf_op jit(solution)/shard_map/dot_general | solution.py:105
  153.5 5.4 %convolution_convert_fusion = bf16[8,8,8,6144]{3,2,1,0:T(8,128)(2,1)} fusion(bf16[8,8,8,512]{3,2,1,0:T(8,128)(2,1)S(1)} %bitcast.61, bf16[1,512,6144]{2,1,0:T(8,128)(2,1)S(1)} %bitcast.60), kind=kOutput, calls=%fused_computation | convolution fusion | flops 3224371200 | bytes 13107200 | tf_op jit(solution)/shard_map/dot_general | solution.py:107
  159.0 280.8 %all-reduce.2.cloned.1.call-done = bf16[8,8,8,6144]{3,2,1,0:T(8,128)(2,1)} async-done(((bf16[8,8,8,6144]{3,2,1,0:T(8,128)(2,1)}), bf16[8,8,8,6144]{3,2,1,0:T(8,128)(2,1)}) %all-reduce.2.cloned.1.call-update) | async-done | bytes 6291472 | tf_op jit(solution)/shard_map/psum | solution.py:110
  439.7 2.1 fusion.43
  441.8 4.0 all-to-all-start.1
  446.2 13.2 %all-to-all-done.1 = bf16[8,8,6144]{2,1,0:T(8,128)(2,1)S(1)} async-done(((bf16[8,8,6144]{2,1,0:T(8,128)(2,1)}), bf16[8,8,6144]{2,1,0:T(8,128)(2,1)S(1)}, u32[]{:S(2)}, u32[]{:S(2)}) %all-to-all-start.1) | async-done | bytes 786464 | tf_op jit(solution)/shard_map/all_to_all | solution.py:112
  459.4 1.1 fusion.1
  (50 shorter events, 2.1 us)
Async XLA Ops:
  6.5 7.2 %copy-start.2 = (bf16[16,512]{1,0:T(8,128)(2,1)S(1)}, bf16[16,512]{1,0:T(8,128)(2,1)}, u32[]{:S(2)}) copy-start(bf16[16,512]{1,0:T(8,128)(2,1)} %param.15) | copy-start | bytes 49156
  6.5 132.5 %all-gather.3.cloned.1.call-start = ((), (), s32[]{:S(2)}) async-start(), calls=%async_computation.3 | async-start | bytes 7077888 | tf_op jit(solution)/shard_map/all_gather | solution.py:102
  17.0 5.4 %copy-start.1 = (bf16[16,512]{1,0:T(8,128)(2,1)S(1)}, bf16[16,512]{1,0:T(8,128)(2,1)}, u32[]{:S(2)}) copy-start(bf16[16,512]{1,0:T(8,128)(2,1)} %param.16) | copy-start | bytes 49156
  22.4 5.9 %copy-start = (bf16[16,6144]{1,0:T(8,128)(2,1)S(1)}, bf16[16,6144]{1,0:T(8,128)(2,1)}, u32[]{:S(2)}) copy-start(bf16[16,6144]{1,0:T(8,128)(2,1)} %param.21) | copy-start | bytes 589828
  22.4 7.2 %copy-start.3 = (bf16[6144]{0:T(1024)(128)(2,1)S(1)}, bf16[6144]{0:T(1024)(128)(2,1)}, u32[]{:S(2)}) copy-start(bf16[6144]{0:T(1024)(128)(2,1)} %param.22) | copy-start | bytes 36868
  47.8 391.9 %all-reduce.2.cloned.1.call-start = ((), (), s32[]{:S(2)}) async-start(), calls=%async_computation.2 | async-start | bytes 12582912 | tf_op jit(solution)/shard_map/psum | solution.py:110
  139.0 8.1 %copy-start.5 = (bf16[64,8,6144]{2,1,0:T(8,128)(2,1)S(1)}, bf16[64,8,6144]{2,1,0:T(8,128)(2,1)}, u32[]{:S(2)}) copy-start(bf16[64,8,6144]{2,1,0:T(8,128)(2,1)} %all-gather.3.cloned.1.call-done) | copy-start | bytes 18874372
  139.0 14.5 %slice-start = ((s8[6291456]{0:T(1024)(128)(4,1)}), s8[4194304]{0:T(1024)(128)(4,1)S(1)}, s32[]{:S(2)}) async-start(s8[6291456]{0:T(1024)(128)(4,1)} %bitcast.59), calls=%async_computation.4 | async-start | bytes 8388608
  147.1 6.4 %slice-start.1 = ((s8[6291456]{0:T(1024)(128)(4,1)}), s8[2097152]{0:T(1024)(128)(4,1)S(1)}, s32[]{:S(2)}) async-start(s8[6291456]{0:T(1024)(128)(4,1)} %bitcast.59), calls=%async_computation.5 | async-start | bytes 4194304
  158.9 286.8 %copy-start.4 = (f32[16,2]{0,1:T(2,128)S(1)}, f32[16,2]{0,1:T(2,128)}, u32[]{:S(2)}) copy-start(f32[16,2]{0,1:T(2,128)} %param.24) | copy-start | bytes 388
  158.9 287.0 %copy-start.6 = (s32[32]{0:T(128)S(1)}, s32[32]{0:T(128)}, u32[]{:S(2)}) copy-start(s32[32]{0:T(128)} %and_select_fusion) | copy-start | bytes 388
  441.8 17.6 %all-to-all-start.1 = ((bf16[8,8,6144]{2,1,0:T(8,128)(2,1)}), bf16[8,8,6144]{2,1,0:T(8,128)(2,1)S(1)}, u32[]{:S(2)}, u32[]{:S(2)}) async-start(bf16[8,8,6144]{2,1,0:T(8,128)(2,1)} %fusion.43), calls=%async_computation.1 | async-start | bytes 1572864 | tf_op jit(solution)/shard_map/all_to_all | solution.py:112
Sparse Core Ops, SparseCore 0:
  47.9 91.0 all-gather.2
  159.1 280.6 all-reduce.1
where the time goes:
time: 468 us; the launch traced here: 467 us
  waiting for transfers between devices  385 us (82%)
  matrix products  28 us (6%)
  blocking collectives  19.8 us (4%)
  between operations  13.6 us (3%)
  local copies, waits for them, and re-layouts  10.6 us (2%)
  other arithmetic  6.18 us (1%)
    psum x1, waiting for transfers between devices, on_device(): lax.psum(partial_out.astype(jnp.bfloat16), ('pool', 'shard'))  281 us
    all_gather x1, waiting for transfers between devices, on_device(): rows_in = lax.all_gather(arrived[None], 'shard', axis=0, tiled=True)  91.2 us
    all_to_all x1, blocking collectives, on_device(): lax.all_to_all(outgoing, 'grp', split_axis=0, concat_axis=0, tiled=True)  16.8 us
    all_to_all x1, waiting for transfers between devices, on_device(): lax.all_to_all(owned.astype(jnp.bfloat16), 'grp', split_axis=0, concat_ax...  13.2 us
  transfers between devices with their start and end apart: 3, of which 3 were waited for; matrix products, arithmetic and copies ran while one was open for 0% of the time, Pallas kernels for 0%

commit v1 on v0

v1 whole, which is shorter than its diff:
```python
import functools

import jax
import jax.numpy as jnp
from jax import lax
from jax.experimental import pallas as pl
from jax.experimental.pallas import tpu as pltpu
from jax.sharding import PartitionSpec as P

HD = 128
TOP = 2
CAP = 8
MESH = pl.DeviceIdType.MESH
F32 = jnp.float32
BF16 = jnp.bfloat16
VMEM = pltpu.VMEM


def attention_kernel(
    lens_ref, q_ref, nk_ref, nv_ref, fork_ref, k_ref, v_ref, o_ref, *, rows, group, prompts
):
    scale = HD ** (-0.5)
    cache_len = k_ref.shape[1]
    q_parts = [q_ref[:, g * HD : (g + 1) * HD] for g in range(group)]
    q = jnp.concatenate(q_parts, axis=0)
    new_key = jnp.concatenate([nk_ref[...].astype(F32)] * group, axis=0)
    new_value = jnp.concatenate([nv_ref[...].astype(F32)] * group, axis=0)
    prompt = jnp.concatenate([fork_ref[...] % prompts] * group, axis=0)
    own = jnp.sum(q.astype(F32) * new_key, axis=1, keepdims=True) * scale
    place = lax.broadcasted_iota(jnp.int32, (rows * group, cache_len), 1)
    masked = []
    top = own
    for p in range(prompts):
        score = (
            lax.dot_general(
                q, k_ref[p], (((1,), (1,)), ((), ())), preferred_element_type=F32
            )
            * scale
        )
        limit = jnp.where(prompt == p, lens_ref[p], 0)
        score = jnp.where(place < limit, score, -1e30)
        masked.append((score, place < limit))
        top = jnp.maximum(top, jnp.max(score, axis=1, keepdims=True))
    own_weight = jnp.exp(own - top)
    total = own_weight
    mixed = own_weight * new_value
    for p in range(prompts):
        score, live = masked[p]
        raw = jnp.where(live, jnp.exp(score - top), 0.0)
        total = total + jnp.sum(raw, axis=1, keepdims=True)
        mixed = mixed + jnp.dot(raw.astype(BF16), v_ref[p], preferred_element_type=F32)
    out = (mixed / total).astype(BF16)
    for g in range(group):
        o_ref[:, g * HD : (g + 1) * HD] = out[g * rows : (g + 1) * rows]


def attention(queries, new_keys, new_values, fork_map, key_cache, value_cache, cache_lengths):
    rows, width = queries.shape
    prompts, cache_len, kv_width = key_cache.shape
    heads = kv_width // HD
    group = width // kv_width
    return pl.pallas_call(
        functools.partial(attention_kernel, rows=rows, group=group, prompts=prompts),
        grid_spec=pltpu.PrefetchScalarGridSpec(
            num_scalar_prefetch=1,
            grid=(heads,),
            in_specs=[
                pl.BlockSpec((rows, group * HD), lambda i, s: (0, i)),
                pl.BlockSpec((rows, HD), lambda i, s: (0, i)),
                pl.BlockSpec((rows, HD), lambda i, s: (0, i)),
                pl.BlockSpec((rows, 1), lambda i, s: (0, 0)),
                pl.BlockSpec((prompts, cache_len, HD), lambda i, s: (0, 0, i)),
                pl.BlockSpec((prompts, cache_len, HD), lambda i, s: (0, 0, i)),
            ],
            out_specs=pl.BlockSpec((rows, group * HD), lambda i, s: (0, i)),
        ),
        out_shape=jax.ShapeDtypeStruct((rows, width), BF16),
        compiler_params=pltpu.CompilerParams(vmem_limit_bytes=32 * 2**20),
    )(
        cache_lengths,
        queries,
        new_keys,
        new_values,
        fork_map.reshape(rows, 1),
        key_cache,
        value_cache,
    )


def landed(ref, sem):
    pltpu.make_async_copy(ref, ref, sem).wait()


class Copies:
    def __init__(self, send_sems, recv_sems):
        self.send_sems, self.recv_sems, self.used = send_sems, recv_sems, 0

    def take(self, count=1):
        first = self.used
        self.used += count
        return first

    def send(self, index, src, dst, device):
        copy = pltpu.make_async_remote_copy(
            src_ref=src,
            dst_ref=dst,
            send_sem=self.send_sems.at[index],
            recv_sem=self.recv_sems.at[index],
            device_id=device,
            device_id_type=MESH,
        )
        copy.start()
        return copy

    def arrived(self, index, ref):
        landed(ref, self.recv_sems.at[index])


SEMS = 80


def expert_kernel(
    att_ref,
    res_ref,
    gain_ref,
    ids_ref,
    gw_ref,
    wg_hbm,
    wu_hbm,
    wd_hbm,
    o_ref,
    wg,
    wu,
    wd,
    ssq,
    hid,
    first,
    xb,
    zb,
    yb,
    h,
    g,
    gate,
    up,
    inner,
    part,
    r1p,
    r1m,
    r2p,
    r2m,
    zr,
    zf,
    q,
    t1p,
    t1m,
    t2p,
    t2m,
    xs,
    xr,
    last,
    send_sems,
    recv_sems,
    load_sems,
):
    c = lax.axis_index("pool")
    grp = lax.axis_index("grp")
    shard = lax.axis_index("shard")
    x, zl = grp // 2, grp % 2
    y, zh = shard // 2, shard % 2
    z = zh * 2 + zl
    rows, width = o_ref.shape
    half = width // 2
    hidden = wg.shape[1]

    def device(px, py, pz, pc=c):
        return (pc, px * 2 + pz % 2, py * 2 + pz // 2)

    def shift(a, d):
        return (a + d + 4) % 4

    other = device(x, y, z, 1 - c)
    y_up, y_down = device(x, shift(y, 1), z), device(x, shift(y, -1), z)
    x_to = [device(shift(x, d), y, z) for d in (1, 2, 3)]
    z_out = [shift(z, d) for d in (1, -1, 2)]
    z_in = [shift(z, d) for d in (-1, 1, 2)]
    z_to = [device(x, y, t) for t in z_out]
    y_of = [y, shift(y, -1), shift(y, 1), shift(y, 2)]
    mine = pl.ds(pl.multiple_of(c * half, half), half)
    theirs = pl.ds(pl.multiple_of((1 - c) * half, half), half)
    mine_hidden = pl.ds(pl.multiple_of(c * hidden, hidden), hidden)

    loads = [
        pltpu.make_async_copy(wg_hbm, wg, load_sems.at[0]),
        pltpu.make_async_copy(wu_hbm, wu, load_sems.at[1]),
        pltpu.make_async_copy(wd_hbm.at[:, mine], wd.at[mine_hidden], load_sems.at[2]),
    ]
    for load in loads:
        load.start()

    barrier = pltpu.get_barrier_semaphore()
    partners = [other, y_up, y_down] + x_to + z_to
    for partner in partners:
        pl.semaphore_signal(barrier, inc=1, device_id=partner, device_id_type=MESH)
    pl.semaphore_wait(barrier, len(partners))

    copies = Copies(send_sems, recv_sems)
    sent = []

    hidden_state = res_ref[:, mine].astype(F32) + att_ref[...].astype(F32)
    hid[...] = hidden_state
    square = jnp.sum(hidden_state * hidden_state, axis=1, keepdims=True)
    ssq[0] = jnp.broadcast_to(square, (rows, HD))
    s_ssq = copies.take()
    sent.append(copies.send(s_ssq, ssq.at[0], ssq.at[1], other))

    slots = xb.shape[0] * rows
    slot = lax.broadcasted_iota(jnp.int32, (rows, slots), 1)
    ids = ids_ref[...]
    pick_a = (ids[:, 0:1] == slot // CAP).astype(F32)
    pick_b = (ids[:, 1:2] == slot // CAP).astype(F32)
    before = (
        lax.broadcasted_iota(jnp.int32, (rows, rows), 1)
        < lax.broadcasted_iota(jnp.int32, (rows, rows), 0)
    ).astype(F32)
    rank = jnp.dot(before, pick_a + pick_b, preferred_element_type=F32)
    here = (rank == (slot % CAP).astype(F32)).astype(F32)
    placing = ((pick_a + pick_b) * here).astype(BF16)
    weighting = (pick_a * gw_ref[:, 0:1] + pick_b * gw_ref[:, 1:2]) * here

    copies.arrived(s_ssq, ssq.at[1])
    meansq = (ssq[0][:, 0:1] + ssq[1][:, 0:1]) / width
    normed = (hidden_state * lax.rsqrt(meansq + 1e-05) * gain_ref[:, mine].astype(F32)).astype(BF16)
    outgoing = lax.dot_general(
        placing, normed, (((0,), (0,)), ((), ())), preferred_element_type=F32
    )
    outgoing = outgoing.astype(BF16)
    for i in range(4):
        first[i] = outgoing[i * rows : (i + 1) * rows]

    s_x = copies.take(3)
    for i, d in enumerate((1, 2, 3)):
        sent.append(copies.send(s_x + i, first.at[shift(x, d)], xb.at[x], x_to[i]))
    xb[x] = first[x]
    s_wd = copies.take()
    sent.append(copies.send(s_wd, wd_hbm.at[:, theirs], wd.at[mine_hidden], other))
    for i, d in enumerate((1, 2, 3)):
        copies.arrived(s_x + i, xb.at[shift(x, -d)])

    def split_pairs(src, dst):
        for part_z in range(2):
            for pair in range(2):
                a = src[2 * pair].astype(F32)[part_z * CAP : (part_z + 1) * CAP]
                b = src[2 * pair + 1].astype(F32)[part_z * CAP : (part_z + 1) * CAP]
                dst[part_z, pair * 16 : (pair + 1) * 16] = jnp.concatenate([a, b], axis=0).astype(
                    BF16
                )

    def join_pairs(src, dst):
        for pair in range(2):
            a = src[0, pair * 16 : (pair + 1) * 16].astype(F32)
            b = src[1, pair * 16 : (pair + 1) * 16].astype(F32)
            dst[2 * pair] = jnp.concatenate([a[:CAP], b[:CAP]], axis=0).astype(BF16)
            dst[2 * pair + 1] = jnp.concatenate([a[CAP:], b[CAP:]], axis=0).astype(BF16)

    split_pairs(xb, zb)

    s_rows = copies.take(4)
    s_inner = copies.take(4)
    s_back = copies.take(3)
    s_last = copies.take()

    tile = 256

    def dots(rows_ref, k, weight_rows, add):
        block = y_of[k]

        @pl.loop(0, hidden // tile)
        def _(n):
            columns = pl.ds(pl.multiple_of(n * tile, tile), tile)
            data = rows_ref[block].reshape(-1, half)
            for weight, total in ((wg, gate), (wu, up)):
                value = jnp.dot(data, weight[weight_rows, columns], preferred_element_type=F32)
                if add:
                    value = value + total[k, :, columns]
                total[k, :, columns] = value

    def share_rows(k):
        return copies.send(s_rows + k, h.at[y_of[k]], g.at[y_of[k]], other)

    def own_half(k):
        dots(h, k, mine, False)

    def other_half(k):
        copies.arrived(s_rows + k, g.at[y_of[k]])
        dots(g, k, theirs, True)
        value = gate[k]
        inner[k, c] = (value / (1.0 + jnp.exp(-value)) * up[k]).astype(BF16)
        return copies.send(s_inner + k, inner.at[k, c], inner.at[k, c], other)

    def project(k):
        copies.arrived(s_inner + k, inner.at[k, 1 - c])
        block = y_of[k]

        @pl.loop(0, half // tile)
        def _(n):
            columns = pl.ds(pl.multiple_of(n * tile, tile), tile)
            value = jnp.dot(inner[k, 0], wd[0:hidden, columns], preferred_element_type=F32)
            value += jnp.dot(
                inner[k, 1], wd[hidden : 2 * hidden, columns], preferred_element_type=F32
            )
            part[block, :, :, columns] = value.astype(BF16).reshape(4, 32, tile)

    def load_wait():
        for load in loads[:2]:
            load.wait()

    def total_of(*refs):
        value = refs[0].astype(F32)
        for ref in refs[1:]:
            value = value + ref.astype(F32)
        return value.astype(BF16)

    def core_zero():
        own = []
        s_z = copies.take(3)
        for k in range(3):
            own.append(copies.send(s_z + k, zb.at[z_out[k] % 2], h.at[y, z], z_to[k]))
        h[y, z] = zb[z % 2]
        order = [z] + z_in
        s_up, s_down = copies.take(4), copies.take(4)
        for j in range(4):
            if j > 0:
                copies.arrived(s_z + j - 1, h.at[y, order[j]])
            block = h.at[y, order[j]]
            own.append(copies.send(s_up + j, block, block, y_up))
            own.append(copies.send(s_down + j, block, block, y_down))
        own.append(share_rows(0))
        s_up2, s_down2 = copies.take(4), copies.take(4)
        for j in range(4):
            copies.arrived(s_up + j, h.at[y_of[1], order[j]])
            block = h.at[y_of[1], order[j], 0:16]
            own.append(copies.send(s_up2 + j, block, block, y_up))
            copies.arrived(s_down + j, h.at[y_of[2], order[j]])
            block = h.at[y_of[2], order[j], 16:32]
            own.append(copies.send(s_down2 + j, block, block, y_down))
            if j == 0:
                load_wait()
                own_half(0)
            if j == 1:
                own.append(other_half(0))
        own.append(share_rows(1))
        own.append(share_rows(2))
        own_half(1)
        own_half(2)
        own.append(other_half(1))
        own.append(other_half(2))
        for j in range(4):
            copies.arrived(s_up2 + j, h.at[y_of[3], order[j], 0:16])
            copies.arrived(s_down2 + j, h.at[y_of[3], order[j], 16:32])
        own.append(share_rows(3))
        own_half(3)
        own.append(other_half(3))

        loads[2].wait()
        copies.arrived(s_wd, wd.at[pl.ds(pl.multiple_of((1 - c) * hidden, hidden), hidden)])
        back = z_out + [z]
        project(3)
        s_up, s_down = copies.take(4), copies.take(4)
        for j in range(4):
            block = part.at[y_of[3], back[j]]
            own.append(copies.send(s_up + j, block.at[0:16], r1p.at[back[j]], y_up))
            own.append(copies.send(s_down + j, block.at[16:32], r1m.at[back[j]], y_down))
        project(2)
        project(1)
        s_up2, s_down2 = copies.take(4), copies.take(4)
        for j in range(4):
            at = back[j]
            copies.arrived(s_up + j, r1p.at[at])
            part[y_of[2], at, 0:16] = total_of(part[y_of[2], at, 0:16], r1p[at])
            own.append(copies.send(s_up2 + j, part.at[y_of[2], at], r2p.at[at], y_up))
            copies.arrived(s_down + j, r1m.at[at])
            part[y_of[1], at, 16:32] = total_of(part[y_of[1], at, 16:32], r1m[at])
            own.append(copies.send(s_down2 + j, part.at[y_of[1], at], r2m.at[at], y_down))
        project(0)
        s_z = copies.take(3)
        for j in range(4):
            at = back[j]
            copies.arrived(s_up2 + j, r2p.at[at])
            copies.arrived(s_down2 + j, r2m.at[at])
            part[y, at] = total_of(part[y, at], r2p[at], r2m[at])
            if j < 3:
                own.append(copies.send(s_z + j, part.at[y, at], zr.at[j], z_to[j]))
        for j in range(3):
            copies.arrived(s_z + j, zr.at[j])
        q[0, z % 2] = total_of(part[y, z], zr[2])
        q[0, 1 - z % 2] = total_of(zr[0], zr[1])
        for copy in own:
            copy.wait_send()

    def core_one():
        own = []
        s_up, s_down = copies.take(), copies.take()
        own.append(copies.send(s_up, zb, yb.at[y], y_up))
        own.append(copies.send(s_down, zb, yb.at[y], y_down))
        s_z = copies.take(12)

        def spread(k, block):
            for j in range(3):
                own.append(
                    copies.send(
                        s_z + 3 * k + j, block.at[z_out[j] % 2], h.at[y_of[k], z], z_to[j]
                    )
                )
            h[y_of[k], z] = block[z % 2]

        def gathered(k):
            for j in range(3):
                copies.arrived(s_z + 3 * k + j, h.at[y_of[k], z_in[j]])

        spread(0, zb)
        s_up2, s_down2 = copies.take(), copies.take()
        copies.arrived(s_up, yb.at[y_of[1]])
        block = yb.at[y_of[1], 0]
        own.append(copies.send(s_up2, block, block, y_up))
        spread(1, yb.at[y_of[1]])
        copies.arrived(s_down, yb.at[y_of[2]])
        block = yb.at[y_of[2], 1]
        own.append(copies.send(s_down2, block, block, y_down))
        spread(2, yb.at[y_of[2]])
        gathered(0)
        own.append(share_rows(0))
        load_wait()
        own_half(0)
        copies.arrived(s_up2, yb.at[y_of[3], 0])
        copies.arrived(s_down2, yb.at[y_of[3], 1])
        spread(3, yb.at[y_of[3]])
        own.append(other_half(0))
        for k in (1, 2, 3):
            gathered(k)
            own.append(share_rows(k))
            own_half(k)
            own.append(other_half(k))

        loads[2].wait()
        copies.arrived(s_wd, wd.at[pl.ds(pl.multiple_of((1 - c) * hidden, hidden), hidden)])
        s_zf = copies.take(12)
        order = (3, 2, 1, 0)
        for k in order:
            project(k)
            for j in range(3):
                own.append(
                    copies.send(s_zf + 3 * k + j, part.at[y_of[k], z_out[j]], zf.at[k, j], z_to[j])
                )
        s_up, s_down = copies.take(), copies.take()
        s_up2, s_down2 = copies.take(), copies.take()
        for k in order:
            for j in range(3):
                copies.arrived(s_zf + 3 * k + j, zf.at[k, j])
            q[k, z % 2] = total_of(part[y_of[k], z], zf[k, 2])
            q[k, 1 - z % 2] = total_of(zf[k, 0], zf[k, 1])
            if k == 3:
                own.append(copies.send(s_up, q.at[3, 0], t1p, y_up))
                own.append(copies.send(s_down, q.at[3, 1], t1m, y_down))
            elif k == 2:
                copies.arrived(s_up, t1p)
                q[2, 0] = total_of(q[2, 0], t1p[...])
                own.append(copies.send(s_up2, q.at[2], t2p, y_up))
            elif k == 1:
                copies.arrived(s_down, t1m)
                q[1, 1] = total_of(q[1, 1], t1m[...])
                own.append(copies.send(s_down2, q.at[1], t2m, y_down))
        copies.arrived(s_up2, t2p)
        copies.arrived(s_down2, t2m)
        q[0] = total_of(q[0], t2p[...], t2m[...])
        for copy in own:
            copy.wait_send()

    common = copies.used
    pl.when(c == 0)(core_zero)
    used_zero, copies.used = copies.used, common
    pl.when(c == 1)(core_one)
    assert max(used_zero, copies.used) <= SEMS

    join_pairs(q.at[0], xs)
    for i, d in enumerate((1, 2, 3)):
        sent.append(copies.send(s_back + i, xs.at[shift(x, d)], xr.at[x], x_to[i]))
    xr[x] = xs[x]
    for i, d in enumerate((1, 2, 3)):
        copies.arrived(s_back + i, xr.at[shift(x, -d)])
    data = xr[...].reshape(slots, half)
    coarse = weighting.astype(BF16)
    fine = (weighting - coarse.astype(F32)).astype(BF16)
    result = jnp.dot(coarse, data, preferred_element_type=F32)
    result += jnp.dot(fine, data, preferred_element_type=F32)
    last[0] = (hid[...] + result).astype(BF16)
    sent.append(copies.send(s_last, last.at[0], last.at[1], other))
    o_ref[:, mine] = last[0]
    copies.arrived(s_last, last.at[1])
    o_ref[:, theirs] = last[1]
    for copy in sent:
        copy.wait_send()


def on_device(
    queries,
    new_keys,
    new_values,
    fork_map,
    key_cache,
    value_cache,
    cache_lengths,
    residual,
    norm_gain,
    expert_ids,
    gate_weights,
    w_gate,
    w_up,
    w_down,
):
    attended = attention(
        queries, new_keys, new_values, fork_map, key_cache, value_cache, cache_lengths
    )
    rows, width = residual.shape
    half = width // 2
    hidden = w_gate.shape[2]
    vmem = pl.BlockSpec(memory_space=VMEM)
    hbm = pl.BlockSpec(memory_space=pl.ANY)
    return pl.pallas_call(
        expert_kernel,
        out_shape=jax.ShapeDtypeStruct((rows, width), BF16),
        in_specs=[vmem] * 5 + [hbm] * 3,
        out_specs=vmem,
        scratch_shapes=[
            VMEM((width, hidden), BF16),
            VMEM((width, hidden), BF16),
            VMEM((2 * hidden, half), BF16),
            VMEM((2, rows, HD), F32),
            VMEM((rows, half), F32),
            VMEM((4, 16, half), BF16),
            VMEM((4, 16, half), BF16),
            VMEM((2, 32, half), BF16),
            VMEM((4, 2, 32, half), BF16),
            VMEM((4, 4, 32, half), BF16),
            VMEM((4, 4, 32, half), BF16),
            VMEM((4, 128, hidden), F32),
            VMEM((4, 128, hidden), F32),
            VMEM((4, 2, 128, hidden), BF16),
            VMEM((4, 4, 32, half), BF16),
            VMEM((4, 16, half), BF16),
            VMEM((4, 16, half), BF16),
            VMEM((4, 32, half), BF16),
            VMEM((4, 32, half), BF16),
            VMEM((3, 32, half), BF16),
            VMEM((4, 3, 32, half), BF16),
            VMEM((4, 2, 32, half), BF16),
            VMEM((32, half), BF16),
            VMEM((32, half), BF16),
            VMEM((2, 32, half), BF16),
            VMEM((2, 32, half), BF16),
            VMEM((4, 16, half), BF16),
            VMEM((4, 16, half), BF16),
            VMEM((2, rows, half), BF16),
            pltpu.SemaphoreType.DMA((SEMS,)),
            pltpu.SemaphoreType.DMA((SEMS,)),
            pltpu.SemaphoreType.DMA((3,)),
        ],
        compiler_params=pltpu.CompilerParams(
            collective_id=0, has_side_effects=True, vmem_limit_bytes=60 * 2**20
        ),
    )(
        attended,
        residual,
        norm_gain.reshape(1, width),
        expert_ids,
        gate_weights,
        w_gate[0],
        w_up[0],
        w_down[0],
    )


def solution(mesh):
    in_specs = (
        P(("grp", "shard"), "pool"),
        P(("grp", "shard"), "pool"),
        P(("grp", "shard"), "pool"),
        P(("grp", "shard")),
        P(("grp", "shard"), None, "pool"),
        P(("grp", "shard"), None, "pool"),
        P(("grp", "shard")),
        P(("grp", "shard"), None),
        P(),
        P(("grp", "shard"), None),
        P(("grp", "shard"), None),
        P("grp", None, ("pool", "shard")),
        P("grp", None, ("pool", "shard")),
        P("grp", ("pool", "shard"), None),
    )
    out_specs = P(("grp", "shard"), None)
    return jax.shard_map(
        on_device, mesh=mesh, in_specs=in_specs, out_specs=out_specs, check_vma=False
    )
```

time: 468 us -> 103 us (0.22)
  waiting for transfers between devices: 385 us -> 0 us
  Pallas kernels: 0 us -> 89.2 us
  matrix products: 28 us -> 0 us
  blocking collectives: 19.8 us -> 0 us
  between operations: 13.6 us -> 0.03 us
  other arithmetic: 6.18 us -> 0 us
    psum x1 -> x0, waiting for transfers between devices: 281 us -> none  [on_device(): lax.psum(partial_out.astype(jnp.bfloat16), ('pool', 'shard'))]
    all_gather x1 -> x0, waiting for transfers between devices: 91.2 us -> none  [on_device(): rows_in = lax.all_gather(arrived[None], 'shard', axis=0, tiled=True)]
    pallas_call x0 -> x2, Pallas kernels: none -> 89.2 us  [the longest x1 84.8 us: on_device(): pl.pallas_call(expert_kernel, out_shape=jax.ShapeDtypeStruct((rows, width...]
    dot_general x10 -> x0, matrix products: 28 us -> none  [the longest x1 8.05 us: on_device(): gate_part = jnp.dot(flat, w_gate[0], preferred_element_type=jnp.float32)]
    all_to_all x1 -> x0, blocking collectives: 16.8 us -> none  [on_device(): lax.all_to_all(outgoing, 'grp', split_axis=0, concat_axis=0, tiled=True)]
    all_to_all x1 -> x0, waiting for transfers between devices: 13.2 us -> none  [on_device(): lax.all_to_all(owned.astype(jnp.bfloat16), 'grp', split_axis=0, concat_ax...]
    unnamed x20 -> x17, local copies, waits for them, and re-layouts: 0.89 us -> 11.1 us
    reshape x4 -> x2, local copies, waits for them, and re-layouts: 8.95 us -> 2.06 us  [the longest x1 1.33 us: on_device(): norm_gain.reshape(1, width)]
  transfers between devices with their start and end apart: 3 -> 0, of which waited for: 3 -> 0; matrix products, arithmetic and copies ran while one was open for 0% -> 0% of each run, Pallas kernels for 0% -> 0%
where the time goes in v1:
time: 103 us; the launch traced here: 102 us
  Pallas kernels  89.2 us (87%)
  local copies, waits for them, and re-layouts  13.2 us (13%)
    pallas_call x1, Pallas kernels, on_device(): pl.pallas_call(expert_kernel, out_shape=jax.ShapeDtypeStruct((rows, width...  84.8 us
    unnamed x17, local copies, waits for them, and re-layouts  11.1 us
    pallas_call x1, Pallas kernels, attention(): pl.pallas_call(functools.partial(attention_kernel, rows=rows, group=group...  4.36 us

profile of v1, /device:TPU:1, one launch (start us, length us, event | category | flops | bytes accessed | tf_op | source)
XLA Modules:
  0.0 102.4 jit_solution(10369260060976523757)
XLA Ops:
  0.0 0.7 copy.15.fork_ref
  0.7 1.4 %copy.16.ids_ref = s32[16,2]{1,0:T(8,128)} copy(s32[16,2]{0,1:T(2,128)} %param.23) | data formatting | bytes 256 | tf_op args[9]
  2.1 1.3 %copy.17.gw_ref = f32[16,2]{1,0:T(8,128)} copy(f32[16,2]{0,1:T(2,128)} %param.24) | data formatting | bytes 256 | tf_op args[10]
  3.4 1.3 %reshape.7.gain_ref = bf16[1,6144]{1,0:T(2,128)(2,1)} reshape(bf16[6144]{0:T(1024)(128)(2,1)} %param.22) | data formatting | bytes 24576 | tf_op jit(solution)/shard_map/reshape | solution.py:573
  4.8 0.0 copy-start
  4.8 1.6 %copy-done = bf16[2,1024,512]{2,1,0:T(8,128)(2,1)S(1)} copy-done((bf16[2,1024,512]{2,1,0:T(8,128)(2,1)S(1)}, bf16[2,1024,512]{2,1,0:T(8,128)(2,1)}, u32[]{:S(2)}) %copy-start) | copy-done | bytes 2097176
  6.4 0.0 copy-start.1
  6.4 1.6 %copy-done.1 = bf16[2,1024,512]{2,1,0:T(8,128)(2,1)S(1)} copy-done((bf16[2,1024,512]{2,1,0:T(8,128)(2,1)S(1)}, bf16[2,1024,512]{2,1,0:T(8,128)(2,1)}, u32[]{:S(2)}) %copy-start.1) | copy-done | bytes 2097176
  7.9 0.0 copy-start.3
  7.9 0.9 copy-done.3
  8.8 0.0 copy-start.4
  8.8 0.7 copy-done.4
  9.6 0.0 copy-start.5
  9.6 0.7 copy-done.5
  10.3 0.0 copy-start.6
  10.3 0.7 copy-done.6
  10.9 4.4 %shard_map.136.att_ref = bf16[16,3072]{1,0:T(8,128)(2,1)S(1)} custom-call(s32[2]{0:T(128)S(1)} %copy-done.6, bf16[16,3072]{1,0:T(8,128)(2,1)S(1)} %copy-done.3, bf16[16,512]{1,0:T(8,128)(2,1)S(1)} %copy-done.4, bf16[16,512]{1,0:T(8,128)(2,1)S(1)} %copy-done.5, s32[16,1]{1,0:T(8,128)S(1)} %copy.15.fork_ref, bf16[2,1024,512]{2,1,0:T(8,128)(2,1)S(1)} %copy-done, ...), custom_call_target="tpu_custom_call" | custom-call | tf_op jit(solution)/shard_map/pallas_call | solution.py:62
  15.3 0.0 copy-start.2
  15.3 0.6 copy-done.2
  15.9 84.8 %shard_map.137 = bf16[16,6144]{1,0:T(8,128)(2,1)} custom-call(bf16[16,3072]{1,0:T(8,128)(2,1)} %copy-done.2, bf16[16,6144]{1,0:T(8,128)(2,1)} %res_ref.1, bf16[1,6144]{1,0:T(2,128)(2,1)} %reshape.7.gain_ref, s32[16,2]{1,0:T(8,128)} %copy.16.ids_ref, f32[16,2]{1,0:T(8,128)} %copy.17.gw_ref, bf16[6144,512]{1,0:T(8,128)(2,1)} %bitcast.4, ...), custom_call_target="tpu_custom_call" | custom-call | tf_op jit(solution)/shard_map/pallas_call | solution.py:528
  100.7 1.6 %copy.19 = bf16[16,6144]{1,0:T(8,128)(2,1)} copy(bf16[16,6144]{1,0:T(8,128)(2,1)} %shard_map.137) | data formatting | bytes 393216
Async XLA Ops:
  4.8 1.6 %copy-start = (bf16[2,1024,512]{2,1,0:T(8,128)(2,1)S(1)}, bf16[2,1024,512]{2,1,0:T(8,128)(2,1)}, u32[]{:S(2)}) copy-start(bf16[2,1024,512]{2,1,0:T(8,128)(2,1)} %k_ref.1) | copy-start | bytes 6291460
  6.4 1.6 %copy-start.1 = (bf16[2,1024,512]{2,1,0:T(8,128)(2,1)S(1)}, bf16[2,1024,512]{2,1,0:T(8,128)(2,1)}, u32[]{:S(2)}) copy-start(bf16[2,1024,512]{2,1,0:T(8,128)(2,1)} %v_ref.1) | copy-start | bytes 6291460
  7.9 0.9 copy-start.3
  8.8 0.7 copy-start.4
  9.6 0.7 copy-start.5
  10.3 0.7 copy-start.6
  15.3 0.6 copy-start.2

commit v2 on v1

v2 whole, which is shorter than its diff:
```python
import math

import jax
import jax.numpy as jnp
from jax import lax
from jax.experimental import pallas as pl
from jax.experimental.pallas import tpu as pltpu
from jax.sharding import PartitionSpec as P

HD = 128
CAP = 8
MESH = pl.DeviceIdType.MESH
F32 = jnp.float32
BF16 = jnp.bfloat16
VMEM = pltpu.VMEM


def landed(ref, sem):
    pltpu.make_async_copy(ref, ref, sem).wait()


class Copies:
    def __init__(self, send_sems, recv_sems):
        self.send_sems, self.recv_sems, self.used = send_sems, recv_sems, 0

    def take(self, count=1):
        first = self.used
        self.used += count
        return first

    def send(self, index, src, dst, device):
        copy = pltpu.make_async_remote_copy(
            src_ref=src,
            dst_ref=dst,
            send_sem=self.send_sems.at[index],
            recv_sem=self.recv_sems.at[index],
            device_id=device,
            device_id_type=MESH,
        )
        copy.start()
        return copy

    def arrived(self, index, ref):
        landed(ref, self.recv_sems.at[index])


SEMS = 80


def layer_kernel(
    lens_ref,
    fork_ref,
    gain_ref,
    ids_ref,
    gw_ref,
    q_hbm,
    nk_hbm,
    nv_hbm,
    k_hbm,
    v_hbm,
    res_hbm,
    wg_hbm,
    wu_hbm,
    wd_hbm,
    o_ref,
    q_in,
    nk_in,
    nv_in,
    k_in,
    v_in,
    res_in,
    wg,
    wu,
    wd,
    ssq,
    hid,
    first,
    xb,
    zb,
    yb,
    h,
    g,
    gate,
    up,
    inner,
    part,
    r1p,
    r1m,
    r2p,
    r2m,
    zr,
    zf,
    q,
    t1p,
    t1m,
    t2p,
    t2m,
    xs,
    xr,
    last,
    send_sems,
    recv_sems,
    load_sems,
):
    c = lax.axis_index("pool")
    grp = lax.axis_index("grp")
    shard = lax.axis_index("shard")
    x, zl = grp // 2, grp % 2
    y, zh = shard // 2, shard % 2
    z = zh * 2 + zl
    rows, width = o_ref.shape
    half = width // 2
    hidden = wg.shape[1]

    def device(px, py, pz, pc=c):
        return (pc, px * 2 + pz % 2, py * 2 + pz // 2)

    def shift(a, d):
        return (a + d + 4) % 4

    other = device(x, y, z, 1 - c)
    y_up, y_down = device(x, shift(y, 1), z), device(x, shift(y, -1), z)
    x_to = [device(shift(x, d), y, z) for d in (1, 2, 3)]
    z_out = [shift(z, d) for d in (1, -1, 2)]
    z_to = [device(x, y, t) for t in z_out]
    mine = pl.ds(pl.multiple_of(c * half, half), half)
    theirs = pl.ds(pl.multiple_of((1 - c) * half, half), half)
    mine_hidden = pl.ds(pl.multiple_of(c * hidden, hidden), hidden)

    def load(index, src, dst):
        copy = pltpu.make_async_copy(src, dst, load_sems.at[index])
        copy.start()
        return copy

    heads = k_in.shape[0]
    group = half // (heads * HD)
    query_loads = [load(0, q_hbm, q_in), load(1, nk_hbm, nk_in), load(2, nv_hbm, nv_in)]
    cache_loads = []
    for head in range(heads):
        columns = slice(head * HD, (head + 1) * HD)
        cache_loads.append(
            (
                load(3 + 2 * head, k_hbm.at[:, :, columns], k_in.at[head]),
                load(4 + 2 * head, v_hbm.at[:, :, columns], v_in.at[head]),
            )
        )
    res_load = load(3 + 2 * heads, res_hbm.at[:, mine], res_in)
    loads = [
        load(4 + 2 * heads, wg_hbm, wg),
        load(5 + 2 * heads, wu_hbm, wu),
        load(6 + 2 * heads, wd_hbm.at[:, mine], wd.at[mine_hidden]),
    ]

    barrier = pltpu.get_barrier_semaphore()
    partners = [other, y_up, y_down] + x_to + z_to
    for partner in partners:
        pl.semaphore_signal(barrier, inc=1, device_id=partner, device_id_type=MESH)

    prompts, cache_len = k_in.shape[1], k_in.shape[2]
    diagonal = lax.broadcasted_iota(jnp.int32, (rows, rows), 0) == lax.broadcasted_iota(
        jnp.int32, (rows, rows), 1
    )
    prompt = jnp.sum(jnp.where(diagonal, fork_ref[...] % prompts, 0), axis=1, keepdims=True)
    prompt = jnp.concatenate([prompt] * group, axis=0)
    place = lax.broadcasted_iota(jnp.int32, (rows * group, cache_len), 1)
    limits = [jnp.where(prompt == p, lens_ref[p], 0) for p in range(prompts)]
    power = HD ** (-0.5) * math.log2(math.e)
    for query_load in query_loads:
        query_load.wait()
    attended = []
    for head in range(heads):
        at = head * group * HD
        queries = jnp.concatenate(
            [q_in[:, at + i * HD : at + (i + 1) * HD] for i in range(group)], axis=0
        )
        new_key = nk_in[:, head * HD : (head + 1) * HD].astype(F32)
        new_value = nv_in[:, head * HD : (head + 1) * HD].astype(F32)
        own = queries.astype(F32) * jnp.concatenate([new_key] * group, axis=0)
        own = jnp.sum(own, axis=1, keepdims=True)
        top = own
        scores = []
        cache_loads[head][0].wait()
        for p in range(prompts):
            score = lax.dot_general(
                queries, k_in[head, p], (((1,), (1,)), ((), ())), preferred_element_type=F32
            )
            score = jnp.where(place < limits[p], score, -1e30)
            scores.append(score)
            top = jnp.maximum(top, jnp.max(score, axis=1, keepdims=True))
        own_weight = jnp.exp2((own - top) * power)
        total = own_weight
        mixed = own_weight * jnp.concatenate([new_value] * group, axis=0)
        cache_loads[head][1].wait()
        for p in range(prompts):
            raw = jnp.exp2((scores[p] - top) * power)
            total = total + jnp.sum(raw, axis=1, keepdims=True)
            mixed = mixed + jnp.dot(
                raw.astype(BF16), v_in[head, p], preferred_element_type=F32
            )
        out = (mixed / total).astype(BF16).astype(F32)
        attended += [out[i * rows : (i + 1) * rows] for i in range(group)]
    attended = jnp.concatenate(attended, axis=1)

    slots = xb.shape[0] * rows
    slot = lax.broadcasted_iota(jnp.int32, (slots, rows), 0)
    pick_a = (ids_ref[0:1] == slot // CAP).astype(F32)
    pick_b = (ids_ref[1:2] == slot // CAP).astype(F32)
    before = (
        lax.broadcasted_iota(jnp.int32, (rows, rows), 0)
        < lax.broadcasted_iota(jnp.int32, (rows, rows), 1)
    ).astype(F32)
    rank = jnp.dot(pick_a + pick_b, before, preferred_element_type=F32)
    here = (rank == (slot % CAP).astype(F32)).astype(F32)
    placing = ((pick_a + pick_b) * here).astype(BF16)
    weighting = (pick_a * gw_ref[0:1] + pick_b * gw_ref[1:2]) * here
    gain = gain_ref[...].astype(F32)
    gain_rows = half // HD
    gain = jnp.where(c == 0, gain[:gain_rows], gain[gain_rows:])

    pl.semaphore_wait(barrier, len(partners))

    copies = Copies(send_sems, recv_sems)
    sent = []

    res_load.wait()
    hidden_state = res_in[...].astype(F32) + attended
    hid[...] = hidden_state
    square = jnp.sum(hidden_state * hidden_state, axis=1, keepdims=True)
    ssq[0] = jnp.broadcast_to(square, (rows, HD))
    s_ssq = copies.take()
    sent.append(copies.send(s_ssq, ssq.at[0], ssq.at[1], other))

    copies.arrived(s_ssq, ssq.at[1])
    meansq = (ssq[0][:, 0:1] + ssq[1][:, 0:1]) / width
    normed = hidden_state * lax.rsqrt(meansq + 1e-05)
    normed = jnp.concatenate(
        [normed[:, i * HD : (i + 1) * HD] * gain[i : i + 1] for i in range(gain_rows)], axis=1
    ).astype(BF16)
    outgoing = jnp.dot(placing, normed, preferred_element_type=F32)
    outgoing = outgoing.astype(BF16)
    for i in range(4):
        first[i] = outgoing[i * rows : (i + 1) * rows]

    s_x = copies.take(3)
    for i, d in enumerate((1, 2, 3)):
        sent.append(copies.send(s_x + i, first.at[shift(x, d)], xb.at[x], x_to[i]))
    xb[x] = first[x]
    def split_pairs(src, dst):
        for part_z in range(2):
            for pair in range(2):
                a = src[2 * pair].astype(F32)[part_z * CAP : (part_z + 1) * CAP]
                b = src[2 * pair + 1].astype(F32)[part_z * CAP : (part_z + 1) * CAP]
                dst[part_z, pair * 16 : (pair + 1) * 16] = jnp.concatenate([a, b], axis=0).astype(
                    BF16
                )

    def join_pairs(src, dst):
        for pair in range(2):
            a = src[0, pair * 16 : (pair + 1) * 16].astype(F32)
            b = src[1, pair * 16 : (pair + 1) * 16].astype(F32)
            dst[2 * pair] = jnp.concatenate([a[:CAP], b[:CAP]], axis=0).astype(BF16)
            dst[2 * pair + 1] = jnp.concatenate([a[CAP:], b[CAP:]], axis=0).astype(BF16)

    s_rows = copies.take(4)
    s_inner = copies.take(4)
    s_back = copies.take(3)
    s_last = copies.take()

    def dots(rows_ref, k, count, weight_rows, add):
        data = rows_ref[k : k + count].reshape(count * 128, half)
        for weight, total in ((wg, gate), (wu, up)):

            @pl.loop(0, hidden // 256)
            def _(n):
                columns = pl.ds(pl.multiple_of(n * 256, 256), 256)
                value = jnp.dot(data, weight[weight_rows, columns], preferred_element_type=F32)
                at = slice(k * 128, (k + count) * 128)
                if add:
                    value = value + total[at, columns]
                total[at, columns] = value

    def share_rows(k):
        return copies.send(s_rows + k, h.at[k], g.at[k], other)

    def own_half(k, count=1):
        dots(h, k, count, mine, False)

    def other_half(k, count=1):
        for i in range(k, k + count):
            copies.arrived(s_rows + i, g.at[i])
        dots(g, k, count, theirs, True)
        at = slice(k * 128, (k + count) * 128)
        value = gate[at]
        inner[c, at] = (value / (1.0 + jnp.exp(-value)) * up[at]).astype(BF16)
        block = inner.at[c, at]
        return copies.send(s_inner + k, block, block, other)

    def project(k, count=1):
        at = slice(k * 128, (k + count) * 128)
        copies.arrived(s_inner + k, inner.at[1 - c, at])

        @pl.loop(0, half // 1024)
        def _(n):
            columns = pl.ds(pl.multiple_of(n * 1024, 1024), 1024)
            value = jnp.dot(inner[0, at], wd[0:hidden, columns], preferred_element_type=F32)
            value += jnp.dot(
                inner[1, at], wd[hidden : 2 * hidden, columns], preferred_element_type=F32
            )
            part[k : k + count, :, :, columns] = value.astype(BF16).reshape(count, 4, 32, 1024)

    wd_pieces = 4
    s_wd = copies.take(wd_pieces)
    piece = hidden // wd_pieces

    def share_wd(i):
        rows_here = pl.ds(pl.multiple_of(c * hidden + i * piece, piece), piece)
        src = wd_hbm.at[i * piece : (i + 1) * piece, theirs]
        return copies.send(s_wd + i, src, wd.at[rows_here], other)

    def wd_wait():
        loads[2].wait()
        for i in range(wd_pieces):
            at = pl.multiple_of((1 - c) * hidden + i * piece, piece)
            copies.arrived(s_wd + i, wd.at[pl.ds(at, piece)])

    sent.append(share_wd(0))
    for i, d in enumerate((1, 2, 3)):
        copies.arrived(s_x + i, xb.at[shift(x, -d)])
    split_pairs(xb, zb)

    def load_wait():
        for load in loads[:2]:
            load.wait()

    def total_of(*refs):
        value = refs[0].astype(F32)
        for ref in refs[1:]:
            value = value + ref.astype(F32)
        return value.astype(BF16)

    def core_zero():
        own = []
        s_z = copies.take(3)
        for k in range(3):
            own.append(copies.send(s_z + k, zb.at[z_out[k] % 2], h.at[0, k + 1], z_to[k]))
        h[0, 0] = zb[z % 2]
        s_up, s_down = copies.take(4), copies.take(4)
        for j in range(4):
            if j > 0:
                copies.arrived(s_z + j - 1, h.at[0, j])
            own.append(copies.send(s_up + j, h.at[0, j], h.at[1, j], y_up))
            own.append(copies.send(s_down + j, h.at[0, j], h.at[2, j], y_down))
        own.append(share_rows(0))
        own.append(share_wd(1))
        s_up2, s_down2 = copies.take(4), copies.take(4)
        for j in range(4):
            copies.arrived(s_up + j, h.at[1, j])
            own.append(copies.send(s_up2 + j, h.at[1, j, 0:16], h.at[3, j, 0:16], y_up))
            copies.arrived(s_down + j, h.at[2, j])
            own.append(copies.send(s_down2 + j, h.at[2, j, 16:32], h.at[3, j, 16:32], y_down))
            if j == 0:
                load_wait()
                own_half(0)
            if j == 1:
                own.append(other_half(0))
                own.append(share_wd(2))
        own.append(share_rows(1))
        own.append(share_rows(2))
        own.append(share_wd(3))
        own_half(1, 2)
        own.append(other_half(1, 2))
        for j in range(4):
            copies.arrived(s_up2 + j, h.at[3, j, 0:16])
            copies.arrived(s_down2 + j, h.at[3, j, 16:32])
        own.append(share_rows(3))
        own_half(3)
        own.append(other_half(3))

        wd_wait()
        project(3)
        s_up, s_down = copies.take(4), copies.take(4)
        back = (2, 1, 3, 0)
        for j, at in enumerate(back):
            own.append(copies.send(s_up + j, part.at[3, at, 0:16], r1p.at[at], y_up))
            own.append(copies.send(s_down + j, part.at[3, at, 16:32], r1m.at[at], y_down))
        project(1, 2)
        s_up2, s_down2 = copies.take(4), copies.take(4)
        for j, at in enumerate(back):
            copies.arrived(s_up + j, r1p.at[at])
            part[2, at, 0:16] = total_of(part[2, at, 0:16], r1p[at])
            own.append(copies.send(s_up2 + j, part.at[2, at], r2p.at[at], y_up))
            copies.arrived(s_down + j, r1m.at[at])
            part[1, at, 16:32] = total_of(part[1, at, 16:32], r1m[at])
            own.append(copies.send(s_down2 + j, part.at[1, at], r2m.at[at], y_down))
        project(0)
        s_z = copies.take(3)
        for j, at in enumerate(back):
            copies.arrived(s_up2 + j, r2p.at[at])
            copies.arrived(s_down2 + j, r2m.at[at])
            part[0, at] = total_of(part[0, at], r2p[at], r2m[at])
            if j < 3:
                own.append(copies.send(s_z + j, part.at[0, at], zr.at[j], z_to[j]))
        for j in range(3):
            copies.arrived(s_z + j, zr.at[j])
        q[0, z % 2] = total_of(part[0, 0], zr[2])
        q[0, 1 - z % 2] = total_of(zr[0], zr[1])
        for copy in own:
            copy.wait_send()

    def core_one():
        own = []
        s_up, s_down = copies.take(), copies.take()
        own.append(copies.send(s_up, zb, yb.at[0], y_up))
        own.append(copies.send(s_down, zb, yb.at[1], y_down))
        s_z = copies.take(12)

        def spread(k, block):
            for j in range(3):
                own.append(
                    copies.send(
                        s_z + 3 * k + j, block.at[z_out[j] % 2], h.at[k, j + 1], z_to[j]
                    )
                )
            h[k, 0] = block[z % 2]

        def gathered(k):
            for j in range(3):
                copies.arrived(s_z + 3 * k + j, h.at[k, j + 1])

        spread(0, zb)
        s_up2, s_down2 = copies.take(), copies.take()
        copies.arrived(s_up, yb.at[0])
        own.append(copies.send(s_up2, yb.at[0, 0], yb.at[2, 0], y_up))
        spread(1, yb.at[0])
        copies.arrived(s_down, yb.at[1])
        own.append(copies.send(s_down2, yb.at[1, 1], yb.at[2, 1], y_down))
        spread(2, yb.at[1])
        gathered(0)
        own.append(share_rows(0))
        own.append(share_wd(1))
        load_wait()
        own_half(0)
        copies.arrived(s_up2, yb.at[2, 0])
        copies.arrived(s_down2, yb.at[2, 1])
        spread(3, yb.at[2])
        own.append(other_half(0))
        own.append(share_wd(2))
        gathered(1)
        own.append(share_rows(1))
        gathered(2)
        own.append(share_rows(2))
        own.append(share_wd(3))
        own_half(1, 2)
        own.append(other_half(1, 2))
        gathered(3)
        own.append(share_rows(3))
        own_half(3)
        own.append(other_half(3))

        wd_wait()
        s_zf = copies.take(12)
        order = (3, 2, 1, 0)

        def spread_back(k):
            for j, at in enumerate((2, 1, 3)):
                own.append(copies.send(s_zf + 3 * k + j, part.at[k, at], zf.at[k, j], z_to[j]))

        project(3)
        spread_back(3)
        project(1, 2)
        spread_back(2)
        spread_back(1)
        project(0)
        spread_back(0)
        s_up, s_down = copies.take(), copies.take()
        s_up2, s_down2 = copies.take(), copies.take()
        for k in order:
            for j in range(3):
                copies.arrived(s_zf + 3 * k + j, zf.at[k, j])
            q[k, z % 2] = total_of(part[k, 0], zf[k, 2])
            q[k, 1 - z % 2] = total_of(zf[k, 0], zf[k, 1])
            if k == 3:
                own.append(copies.send(s_up, q.at[3, 0], t1p, y_up))
                own.append(copies.send(s_down, q.at[3, 1], t1m, y_down))
            elif k == 2:
                copies.arrived(s_up, t1p)
                q[2, 0] = total_of(q[2, 0], t1p[...])
                own.append(copies.send(s_up2, q.at[2], t2p, y_up))
            elif k == 1:
                copies.arrived(s_down, t1m)
                q[1, 1] = total_of(q[1, 1], t1m[...])
                own.append(copies.send(s_down2, q.at[1], t2m, y_down))
        copies.arrived(s_up2, t2p)
        copies.arrived(s_down2, t2m)
        q[0] = total_of(q[0], t2p[...], t2m[...])
        for copy in own:
            copy.wait_send()

    common = copies.used
    pl.when(c == 0)(core_zero)
    used_zero, copies.used = copies.used, common
    pl.when(c == 1)(core_one)
    assert max(used_zero, copies.used) <= SEMS

    join_pairs(q.at[0], xs)
    for i, d in enumerate((1, 2, 3)):
        sent.append(copies.send(s_back + i, xs.at[shift(x, d)], xr.at[x], x_to[i]))
    xr[x] = xs[x]
    for i, d in enumerate((1, 2, 3)):
        copies.arrived(s_back + i, xr.at[shift(x, -d)])
    data = xr[...].reshape(slots, half)
    coarse = weighting.astype(BF16)
    fine = (weighting - coarse.astype(F32)).astype(BF16)
    over_slots = (((0,), (0,)), ((), ()))
    result = lax.dot_general(coarse, data, over_slots, preferred_element_type=F32)
    result += lax.dot_general(fine, data, over_slots, preferred_element_type=F32)
    last[0] = (hid[...] + result).astype(BF16)
    sent.append(copies.send(s_last, last.at[0], last.at[1], other))
    o_ref[:, mine] = last[0]
    copies.arrived(s_last, last.at[1])
    o_ref[:, theirs] = last[1]
    for copy in sent:
        copy.wait_send()


def on_device(
    queries,
    new_keys,
    new_values,
    fork_map,
    key_cache,
    value_cache,
    cache_lengths,
    residual,
    norm_gain,
    expert_ids,
    gate_weights,
    w_gate,
    w_up,
    w_down,
):
    rows, width = residual.shape
    half = width // 2
    hidden = w_gate.shape[2]
    prompts, cache_len, kv_width = key_cache.shape
    heads = kv_width // HD
    vmem = pl.BlockSpec(memory_space=VMEM)
    hbm = pl.BlockSpec(memory_space=pl.ANY)
    return pl.pallas_call(
        layer_kernel,
        out_shape=jax.ShapeDtypeStruct((rows, width), BF16),
        in_specs=[pl.BlockSpec(memory_space=pltpu.SMEM)] + [vmem] * 4 + [hbm] * 9,
        out_specs=vmem,
        scratch_shapes=[
            VMEM((rows, half), BF16),
            VMEM((rows, kv_width), BF16),
            VMEM((rows, kv_width), BF16),
            VMEM((heads, prompts, cache_len, HD), BF16),
            VMEM((heads, prompts, cache_len, HD), BF16),
            VMEM((rows, half), BF16),
            VMEM((width, hidden), BF16),
            VMEM((width, hidden), BF16),
            VMEM((2 * hidden, half), BF16),
            VMEM((2, rows, HD), F32),
            VMEM((rows, half), F32),
            VMEM((4, 16, half), BF16),
            VMEM((4, 16, half), BF16),
            VMEM((2, 32, half), BF16),
            VMEM((3, 2, 32, half), BF16),
            VMEM((4, 4, 32, half), BF16),
            VMEM((4, 4, 32, half), BF16),
            VMEM((512, hidden), F32),
            VMEM((512, hidden), F32),
            VMEM((2, 512, hidden), BF16),
            VMEM((4, 4, 32, half), BF16),
            VMEM((4, 16, half), BF16),
            VMEM((4, 16, half), BF16),
            VMEM((4, 32, half), BF16),
            VMEM((4, 32, half), BF16),
            VMEM((3, 32, half), BF16),
            VMEM((4, 3, 32, half), BF16),
            VMEM((4, 2, 32, half), BF16),
            VMEM((32, half), BF16),
            VMEM((32, half), BF16),
            VMEM((2, 32, half), BF16),
            VMEM((2, 32, half), BF16),
            VMEM((4, 16, half), BF16),
            VMEM((4, 16, half), BF16),
            VMEM((2, rows, half), BF16),
            pltpu.SemaphoreType.DMA((SEMS,)),
            pltpu.SemaphoreType.DMA((SEMS,)),
            pltpu.SemaphoreType.DMA((7 + 2 * heads,)),
        ],
        compiler_params=pltpu.CompilerParams(
            collective_id=0, has_side_effects=True, vmem_limit_bytes=60 * 2**20
        ),
    )(
        cache_lengths,
        fork_map.reshape(1, rows),
        norm_gain.reshape(width // HD, HD),
        expert_ids.T,
        gate_weights.T,
        queries,
        new_keys,
        new_values,
        key_cache,
        value_cache,
        residual,
        w_gate[0],
        w_up[0],
        w_down[0],
    )


def solution(mesh):
    in_specs = (
        P(("grp", "shard"), "pool"),
        P(("grp", "shard"), "pool"),
        P(("grp", "shard"), "pool"),
        P(("grp", "shard")),
        P(("grp", "shard"), None, "pool"),
        P(("grp", "shard"), None, "pool"),
        P(("grp", "shard")),
        P(("grp", "shard"), None),
        P(),
        P(("grp", "shard"), None),
        P(("grp", "shard"), None),
        P("grp", None, ("pool", "shard")),
        P("grp", None, ("pool", "shard")),
        P("grp", ("pool", "shard"), None),
    )
    out_specs = P(("grp", "shard"), None)
    return jax.shard_map(
        on_device, mesh=mesh, in_specs=in_specs, out_specs=out_specs, check_vma=False
    )
```

time: 103 us -> 87.5 us (0.85)
  local copies, waits for them, and re-layouts: 13.2 us -> 1.62 us
  Pallas kernels: 89.2 us -> 85.7 us
    unnamed x17 -> x1, local copies, waits for them, and re-layouts: 11.1 us -> 1.62 us
    pallas_call x2 -> x1, Pallas kernels: 89.2 us -> 85.7 us  [on_device(): pl.pallas_call(layer_kernel, out_shape=jax.ShapeDtypeStruct((rows, width)...]
    reshape x2 -> x0, local copies, waits for them, and re-layouts: 2.06 us -> none  [the longest x1 1.33 us: on_device(): norm_gain.reshape(1, width)]
where the time goes in v2:
time: 87.5 us; the launch traced here: 87.3 us
  Pallas kernels  85.7 us (98%)
  local copies, waits for them, and re-layouts  1.62 us (2%)
    pallas_call x1, Pallas kernels, on_device(): pl.pallas_call(layer_kernel, out_shape=jax.ShapeDtypeStruct((rows, width)...  85.7 us

profile of v2, /device:TPU:1, one launch (start us, length us, event | category | flops | bytes accessed | tf_op | source)
XLA Modules:
  0.0 87.3 jit_solution(2621603636362367746)
XLA Ops:
  0.0 85.7 %shard_map.136 = bf16[16,6144]{1,0:T(8,128)(2,1)} custom-call(s32[2]{0:T(128)} %lens_ref.1, s32[1,16]{1,0:T(1,128)} %bitcast.13, bf16[48,128]{1,0:T(8,128)(2,1)} %bitcast.10, s32[2,16]{1,0:T(2,128)} %bitcast.11, f32[2,16]{1,0:T(2,128)} %bitcast.12, bf16[16,3072]{1,0:T(8,128)(2,1)} %q_hbm.1, bf16[16,512]{1,0:T(8,128)(2,1)} %nk_hbm.1, bf16[16,512]{1,0:T(8,128)(2,1)} %nv_hbm.1, ...), custom_call_target="tpu_custom_call" | custom-call | tf_op jit(solution)/shard_map/pallas_call | solution.py:549
  85.7 1.6 %copy.16 = bf16[16,6144]{1,0:T(8,128)(2,1)} copy(bf16[16,6144]{1,0:T(8,128)(2,1)} %shard_map.136) | data formatting | bytes 393216

commit v3 on v2

v3 whole, which is shorter than its diff:
```python
import math

import jax
import jax.numpy as jnp
from jax import lax
from jax.experimental import pallas as pl
from jax.experimental.pallas import tpu as pltpu
from jax.sharding import PartitionSpec as P

HD = 128
CAP = 8
MESH = pl.DeviceIdType.MESH
F32 = jnp.float32
BF16 = jnp.bfloat16
VMEM = pltpu.VMEM


def landed(ref, sem):
    pltpu.make_async_copy(ref, ref, sem).wait()


class Copies:
    def __init__(self, send_sems, recv_sems):
        self.send_sems, self.recv_sems, self.used = send_sems, recv_sems, 0

    def take(self, count=1):
        first = self.used
        self.used += count
        return first

    def send(self, index, src, dst, device):
        copy = pltpu.make_async_remote_copy(
            src_ref=src,
            dst_ref=dst,
            send_sem=self.send_sems.at[index],
            recv_sem=self.recv_sems.at[index],
            device_id=device,
            device_id_type=MESH,
        )
        copy.start()
        return copy

    def arrived(self, index, ref):
        landed(ref, self.recv_sems.at[index])


SEMS = 112
WIDE = 2048


def layer_kernel(
    lens_ref,
    fork_ref,
    gain_ref,
    ids_ref,
    gw_ref,
    q_hbm,
    nk_hbm,
    nv_hbm,
    k_hbm,
    v_hbm,
    res_hbm,
    wg_hbm,
    wu_hbm,
    wd_hbm,
    o_ref,
    q_in,
    nk_in,
    nv_in,
    k_in,
    v_in,
    res_in,
    wg,
    wu,
    wd,
    ssq,
    hid,
    gate,
    up,
    inner,
    last,
    e_first,
    e_x,
    e_z,
    e_rows,
    e_part,
    e_up,
    e_down,
    e_up2,
    e_down2,
    e_zin,
    e_sum,
    e_back,
    e_end,
    f_first,
    f_x,
    f_z,
    f_y,
    f_rows,
    f_part,
    f_zin,
    f_sum,
    f_up,
    f_down,
    f_up2,
    f_down2,
    f_back,
    f_end,
    d_raw,
    d_weights,
    d_slots,
    d_rows,
    d_part,
    d_xin,
    d_group,
    d_zin,
    d_sum,
    d_yin,
    send_sems,
    recv_sems,
    load_sems,
    turn,
):
    c = lax.axis_index("pool")
    grp = lax.axis_index("grp")
    shard = lax.axis_index("shard")
    x, zl = grp // 2, grp % 2
    y, zh = shard // 2, shard % 2
    z = zh * 2 + zl
    rows, width = o_ref.shape
    half = width // 2
    hidden = wg.shape[1]

    def device(px, py, pz, pc=c):
        return (pc, px * 2 + pz % 2, py * 2 + pz // 2)

    def shift(a, d):
        return (a + d + 4) % 4

    other = device(x, y, z, 1 - c)
    x_out, y_out, z_out = ([shift(a, d) for d in (1, -1, 2)] for a in (x, y, z))
    x_to = [device(t, y, z) for t in x_out]
    y_to = [device(x, t, z) for t in y_out]
    z_to = [device(x, y, t) for t in z_out]
    y_up, y_down = y_to[:2]
    home = (1, 0, 2)
    mine = pl.ds(pl.multiple_of(c * half, half), half)
    theirs = pl.ds(pl.multiple_of((1 - c) * half, half), half)
    mine_hidden = pl.ds(pl.multiple_of(c * hidden, hidden), hidden)

    def load(index, src, dst):
        copy = pltpu.make_async_copy(src, dst, load_sems.at[index])
        copy.start()
        return copy

    heads = k_in.shape[0]
    group = half // (heads * HD)
    query_loads = [load(0, q_hbm, q_in), load(1, nk_hbm, nk_in), load(2, nv_hbm, nv_in)]
    cache_loads = []
    for head in range(heads):
        columns = slice(head * HD, (head + 1) * HD)
        cache_loads.append(
            (
                load(3 + 2 * head, k_hbm.at[:, :, columns], k_in.at[head]),
                load(4 + 2 * head, v_hbm.at[:, :, columns], v_in.at[head]),
            )
        )
    res_load = load(3 + 2 * heads, res_hbm.at[:, mine], res_in)
    loads = [
        load(4 + 2 * heads, wg_hbm, wg),
        load(5 + 2 * heads, wu_hbm, wu),
        load(6 + 2 * heads, wd_hbm.at[:, mine], wd.at[mine_hidden]),
    ]

    barrier = pltpu.get_barrier_semaphore()
    partners = [other] + x_to + y_to + z_to
    for partner in partners:
        pl.semaphore_signal(barrier, inc=1, device_id=partner, device_id_type=MESH)

    prompts, cache_len = k_in.shape[1], k_in.shape[2]
    diagonal = lax.broadcasted_iota(jnp.int32, (rows, rows), 0) == lax.broadcasted_iota(
        jnp.int32, (rows, rows), 1
    )
    prompt = jnp.sum(jnp.where(diagonal, fork_ref[...] % prompts, 0), axis=1, keepdims=True)
    prompt = jnp.concatenate([prompt] * group, axis=0)
    place = lax.broadcasted_iota(jnp.int32, (rows * group, cache_len), 1)
    limits = [jnp.where(prompt == p, lens_ref[p], 0) for p in range(prompts)]
    power = HD ** (-0.5) * math.log2(math.e)
    for query_load in query_loads:
        query_load.wait()
    attended = []
    for head in range(heads):
        at = head * group * HD
        queries = jnp.concatenate(
            [q_in[:, at + i * HD : at + (i + 1) * HD] for i in range(group)], axis=0
        )
        new_key = nk_in[:, head * HD : (head + 1) * HD].astype(F32)
        new_value = nv_in[:, head * HD : (head + 1) * HD].astype(F32)
        own = queries.astype(F32) * jnp.concatenate([new_key] * group, axis=0)
        own = jnp.sum(own, axis=1, keepdims=True)
        top = own
        scores = []
        cache_loads[head][0].wait()
        for p in range(prompts):
            score = lax.dot_general(
                queries, k_in[head, p], (((1,), (1,)), ((), ())), preferred_element_type=F32
            )
            score = jnp.where(place < limits[p], score, -1e30)
            scores.append(score)
            top = jnp.maximum(top, jnp.max(score, axis=1, keepdims=True))
        own_weight = jnp.exp2((own - top) * power)
        total = own_weight
        mixed = own_weight * jnp.concatenate([new_value] * group, axis=0)
        cache_loads[head][1].wait()
        for p in range(prompts):
            raw = jnp.exp2((scores[p] - top) * power)
            total = total + jnp.sum(raw, axis=1, keepdims=True)
            mixed = mixed + jnp.dot(
                raw.astype(BF16), v_in[head, p], preferred_element_type=F32
            )
        out = (mixed / total).astype(BF16).astype(F32)
        attended += [out[i * rows : (i + 1) * rows] for i in range(group)]
    attended = jnp.concatenate(attended, axis=1)

    slots = 4 * rows
    slot = lax.broadcasted_iota(jnp.int32, (slots, rows), 0)
    pick_a = (ids_ref[0:1] == slot // CAP).astype(F32)
    pick_b = (ids_ref[1:2] == slot // CAP).astype(F32)
    before = (
        lax.broadcasted_iota(jnp.int32, (rows, rows), 0)
        < lax.broadcasted_iota(jnp.int32, (rows, rows), 1)
    ).astype(F32)
    rank = jnp.dot(pick_a + pick_b, before, preferred_element_type=F32)
    here = (rank == (slot % CAP).astype(F32)).astype(F32)
    placing = ((pick_a + pick_b) * here).astype(BF16)
    weighting = (pick_a * gw_ref[0:1] + pick_b * gw_ref[1:2]) * here
    coarse = weighting.astype(BF16)
    fine = (weighting - coarse.astype(F32)).astype(BF16)
    gain = gain_ref[...].astype(F32)
    gain_rows = half // HD
    gain = jnp.where(c == 0, gain[:gain_rows], gain[gain_rows:])

    pl.semaphore_wait(barrier, len(partners))

    copies = Copies(send_sems, recv_sems)
    sent = []

    res_load.wait()
    hidden_state = res_in[...].astype(F32) + attended
    hid[...] = hidden_state
    square = jnp.sum(hidden_state * hidden_state, axis=1, keepdims=True)
    ssq[0] = jnp.broadcast_to(square, (rows, HD))
    s_ssq = copies.take()
    sent.append(copies.send(s_ssq, ssq.at[0], ssq.at[1], other))

    copies.arrived(s_ssq, ssq.at[1])
    meansq = (ssq[0][:, 0:1] + ssq[1][:, 0:1]) / width
    normed = hidden_state * lax.rsqrt(meansq + 1e-05)
    normed = jnp.concatenate(
        [normed[:, i * HD : (i + 1) * HD] * gain[i : i + 1] for i in range(gain_rows)], axis=1
    ).astype(BF16)
    over_rows = (((0,), (0,)), ((), ()))
    s_e, s_f, s_d = copies.take(4), copies.take(4), copies.take(4)
    s_inner = copies.take(4)
    s_last = copies.take()
    s_wd = copies.take()

    def split_pairs(src, dst):
        for part_z in range(2):
            for pair in range(2):
                a = src[2 * pair].astype(F32)[part_z * CAP : (part_z + 1) * CAP]
                b = src[2 * pair + 1].astype(F32)[part_z * CAP : (part_z + 1) * CAP]
                dst[part_z, pair * 16 : (pair + 1) * 16] = jnp.concatenate([a, b], axis=0).astype(
                    BF16
                )

    def join_pairs(src, dst):
        for pair in range(2):
            a = src[0, pair * 16 : (pair + 1) * 16].astype(F32)
            b = src[1, pair * 16 : (pair + 1) * 16].astype(F32)
            dst[2 * pair] = jnp.concatenate([a[:CAP], b[:CAP]], axis=0).astype(BF16)
            dst[2 * pair + 1] = jnp.concatenate([a[CAP:], b[CAP:]], axis=0).astype(BF16)

    def dots(data, weight_rows, put):
        for weight, total in ((wg, gate), (wu, up)):

            @pl.loop(0, hidden // 256)
            def _(n):
                columns = pl.ds(pl.multiple_of(n * 256, 256), 256)
                value = jnp.dot(data, weight[weight_rows, columns], preferred_element_type=F32)
                put(total, columns, value)

    def add_chunk(data, weight_rows, k, count):
        at = slice(k * 128, (k + count) * 128)

        def put(total, columns, value):
            total[at, columns] += value

        dots(data, weight_rows, put)

    def add_e(k, count=1):
        add_chunk(e_rows[k : k + count].reshape(count * 128, half), slice(0, half), k, count)

    def add_f(k, count=1):
        data = f_rows[k : k + count].reshape(count * 128, half - WIDE)
        add_chunk(data, slice(half + WIDE, width), k, count)

    def add_d(k, count=1):
        def put(total, columns, value):
            for i in range(count * 16):
                kz, kx, ky = k + i // 16, i // 4 % 4, i % 4
                at = kz * 128 + ky * 32 + kx * CAP
                total[at : at + CAP, columns] += value[i * CAP : (i + 1) * CAP]

        dots(d_rows[k : k + count].reshape(count * 128, WIDE), slice(half, half + WIDE), put)

    def share(first, ref, k):
        return copies.send(first + k, ref.at[k], ref.at[k], other)

    def shared(first, ref, k, count=1):
        for i in range(k, k + count):
            copies.arrived(first + i, ref.at[i])

    def share_wd():
        src = wd_hbm.at[:, theirs]
        return [copies.send(s_wd, src, wd.at[mine_hidden], other)]

    def wd_wait():
        loads[2].wait()
        at = pl.multiple_of((1 - c) * hidden, hidden)
        copies.arrived(s_wd, wd.at[pl.ds(at, hidden)])

    def load_wait():
        for load in loads[:2]:
            load.wait()

    def clear():
        gate[...] = jnp.zeros_like(gate)
        up[...] = jnp.zeros_like(up)

    def activate(k, count=1):
        at = slice(k * 128, (k + count) * 128)
        value = gate[at]
        inner[c, at] = (value / (1.0 + jnp.exp(-value)) * up[at]).astype(BF16)
        return copies.send(s_inner + k, inner.at[c, at], inner.at[c, at], other)

    def inner_wait(k, count=1):
        at = slice(k * 128, (k + count) * 128)
        copies.arrived(s_inner + k, inner.at[1 - c, at])

    def project(k, count, start, stop, put):
        at = slice(k * 128, (k + count) * 128)

        @pl.loop(0, (stop - start) // 1024)
        def _(n):
            columns = pl.ds(pl.multiple_of(start + n * 1024, 1024), 1024)
            value = jnp.dot(inner[0, at], wd[0:hidden, columns], preferred_element_type=F32)
            value += jnp.dot(
                inner[1, at], wd[hidden : 2 * hidden, columns], preferred_element_type=F32
            )
            put(n, value)

    def total_of(*refs):
        value = refs[0].astype(F32)
        for ref in refs[1:]:
            value = value + ref.astype(F32)
        return value.astype(BF16)

    def x_send(first, src, dst):
        done = []
        for i in range(3):
            done.append(copies.send(first + i, src.at[x_out[i]], dst.at[i + 1], x_to[i]))
        dst[0] = src[x]
        return done

    def x_return(first, src, dst):
        done = []
        for i in range(3):
            done.append(copies.send(first + i, src.at[i + 1], dst.at[x], x_to[home[i]]))
        dst[x] = src[0]
        return done

    def x_returned(first, dst):
        for i, d in enumerate((1, -1, 2)):
            copies.arrived(first + i, dst.at[shift(x, d)])

    def weighted(data):
        value = lax.dot_general(coarse, data, over_rows, preferred_element_type=F32)
        return value + lax.dot_general(fine, data, over_rows, preferred_element_type=F32)

    def place_slots(columns):
        return jnp.dot(placing, columns, preferred_element_type=F32).astype(BF16)

    def core_zero():
        own = []
        outgoing = place_slots(normed)
        for i in range(4):
            e_first[i] = outgoing[i * rows : (i + 1) * rows]
        s_x = copies.take(3)
        own += x_send(s_x, e_first, e_x)
        own += share_wd()
        clear()
        for i in range(3):
            copies.arrived(s_x + i, e_x.at[i + 1])
        split_pairs(e_x, e_z)
        s_z = copies.take(3)

        def to_z(k):
            return copies.send(s_z + k, e_z.at[z_out[k] % 2], e_rows.at[k + 1, 0], z_to[k])

        first_z = [to_z(0), to_z(1)]
        e_rows[0, 0] = e_z[z % 2]
        straight, straight_back = (0, 3), (3,)
        s_up, s_down, s_up2, s_down2 = (copies.take(4) for _ in range(4))

        def ring(j):
            if j > 0:
                copies.arrived(s_z + j - 1, e_rows.at[j, 0])
            own.append(copies.send(s_up + j, e_rows.at[j, 0], e_rows.at[j, 1], y_up))
            own.append(copies.send(s_down + j, e_rows.at[j, 0], e_rows.at[j, 2], y_down))
            if j in straight:
                own.append(copies.send(s_up2 + j, e_rows.at[j, 0], e_rows.at[j, 3], y_to[2]))

        def forward(j):
            if j in straight:
                return
            copies.arrived(s_up + j, e_rows.at[j, 1])
            own.append(
                copies.send(s_up2 + j, e_rows.at[j, 1, 0:16], e_rows.at[j, 3, 0:16], y_up)
            )
            copies.arrived(s_down + j, e_rows.at[j, 2])
            own.append(
                copies.send(s_down2 + j, e_rows.at[j, 2, 16:32], e_rows.at[j, 3, 16:32], y_down)
            )

        def ringed(j):
            if j in straight:
                copies.arrived(s_up + j, e_rows.at[j, 1])
                copies.arrived(s_down + j, e_rows.at[j, 2])
                copies.arrived(s_up2 + j, e_rows.at[j, 3])
            else:
                copies.arrived(s_up2 + j, e_rows.at[j, 3, 0:16])
                copies.arrived(s_down2 + j, e_rows.at[j, 3, 16:32])
            own.append(share(s_e, e_rows, j))

        s_bup, s_bdown, s_bup2, s_bdown2 = (copies.take(4) for _ in range(4))
        s_bz = copies.take(3)

        def project_e(k, count=1):
            inner_wait(k, count)

            def put(n, value):
                columns = pl.ds(pl.multiple_of(n * 1024, 1024), 1024)
                value = value.astype(BF16).reshape(count, 4, 32, 1024)
                e_part[k : k + count, :, :, columns] = value

            project(k, count, 0, half, put)
            for j in range(k, k + count):
                far_up, far_down = (y_to[2], y_to[2]) if j in straight_back else (y_up, y_down)
                own.append(copies.send(s_bup + j, e_part.at[j, 3, 0:16], e_up.at[j], far_up))
                own.append(
                    copies.send(s_bdown + j, e_part.at[j, 3, 16:32], e_down.at[j], far_down)
                )
                if j in straight_back:
                    own.append(copies.send(s_bup2 + j, e_part.at[j, 2], e_up2.at[j], y_up))
                    own.append(copies.send(s_bdown2 + j, e_part.at[j, 1], e_down2.at[j], y_down))

        def ring_back(j):
            if j in straight_back:
                return
            copies.arrived(s_bup + j, e_up.at[j])
            e_part[j, 2, 0:16] = total_of(e_part[j, 2, 0:16], e_up[j])
            own.append(copies.send(s_bup2 + j, e_part.at[j, 2], e_up2.at[j], y_up))
            copies.arrived(s_bdown + j, e_down.at[j])
            e_part[j, 1, 16:32] = total_of(e_part[j, 1, 16:32], e_down[j])
            own.append(copies.send(s_bdown2 + j, e_part.at[j, 1], e_down2.at[j], y_down))

        def ringed_back(j):
            copies.arrived(s_bup2 + j, e_up2.at[j])
            copies.arrived(s_bdown2 + j, e_down2.at[j])
            if j in straight_back:
                copies.arrived(s_bup + j, e_up.at[j])
                copies.arrived(s_bdown + j, e_down.at[j])
                e_part[j, 0, 0:16] = total_of(
                    e_part[j, 0, 0:16], e_up2[j, 0:16], e_down2[j, 0:16], e_up[j]
                )
                e_part[j, 0, 16:32] = total_of(
                    e_part[j, 0, 16:32], e_up2[j, 16:32], e_down2[j, 16:32], e_down[j]
                )
            else:
                e_part[j, 0] = total_of(e_part[j, 0], e_up2[j], e_down2[j])
            if j > 0:
                i = j - 1
                own.append(copies.send(s_bz + i, e_part.at[j, 0], e_zin.at[i], z_to[home[i]]))

        ring(0)
        for copy in first_z:
            copy.wait_send()
        last_z = to_z(2)
        forward(0)
        last_z.wait_send()
        pl.semaphore_signal(turn, inc=1, device_id=other, device_id_type=MESH)
        ring(1)
        ring(2)
        ringed(0)
        ring(3)
        load_wait()
        add_e(0)
        shared(s_d, d_rows, 0)
        add_d(0)
        shared(s_f, f_rows, 0)
        add_f(0)
        own.append(activate(0))
        forward(1)
        forward(2)
        wd_wait()
        project_e(0)
        forward(3)
        shared(s_d, d_rows, 1, 2)
        add_d(1, 2)
        shared(s_f, f_rows, 1, 2)
        add_f(1, 2)
        ringed(1)
        ringed(2)
        add_e(1, 2)
        own.append(activate(1, 2))
        ring_back(0)
        ringed(3)
        shared(s_d, d_rows, 3)
        add_d(3)
        shared(s_f, f_rows, 3)
        add_f(3)
        project_e(1, 2)
        add_e(3)
        own.append(activate(3))
        ring_back(1)
        ring_back(2)
        project_e(3)
        ringed_back(0)
        ringed_back(1)
        ringed_back(2)
        ring_back(3)
        ringed_back(3)
        for j in range(3):
            copies.arrived(s_bz + j, e_zin.at[j])
        e_sum[z % 2] = total_of(e_part[0, 0], e_zin[2])
        e_sum[1 - z % 2] = total_of(e_zin[0], e_zin[1])
        join_pairs(e_sum, e_back)
        s_x = copies.take(3)
        own += x_return(s_x, e_back, e_end)
        x_returned(s_x, e_end)
        last[...] = (hid[...] + weighted(e_end[...].reshape(slots, half))).astype(BF16)
        pltpu.make_async_copy(last, o_ref.at[:, mine], load_sems.at[0]).start()
        own.append(copies.send(s_last, last, o_ref.at[:, mine], other))
        for copy in own:
            copy.wait_send()

    def core_one():
        own = []
        eye = diagonal.astype(BF16)
        over_slots = (((1,), (1,)), ((), ()))
        for i, lanes in enumerate((coarse, fine)):
            lanes = lax.dot_general(eye, lanes, over_slots, preferred_element_type=F32)
            d_raw[0, 0, :, WIDE + i * slots : WIDE + (i + 1) * slots] = lanes.astype(BF16)
        d_raw[0, 0, :, 0:WIDE] = normed[:, 0:WIDE]
        s_dy, s_dz = copies.take(3), copies.take(12)
        for i in range(3):
            own.append(copies.send(s_dy + i, d_raw.at[0, 0], d_raw.at[0, i + 1], y_to[i]))

        def raw_to_z(ky, targets):
            for i in targets:
                own.append(
                    copies.send(
                        s_dz + 3 * ky + i, d_raw.at[0, ky], d_raw.at[i + 1, ky], z_to[i]
                    )
                )

        raw_to_z(0, (0, 1))
        outgoing = place_slots(normed[:, WIDE:])
        for i in range(4):
            f_first[i] = outgoing[i * rows : (i + 1) * rows]
        s_x = copies.take(3)
        own += x_send(s_x, f_first, f_x)
        own += share_wd()
        clear()
        for ky in (1, 2, 3):
            copies.arrived(s_dy + ky - 1, d_raw.at[0, ky])
            raw_to_z(ky, (0, 1))

        group_slots = 4 * 4 * CAP
        slot_in = lax.broadcasted_iota(jnp.int32, (slots, group_slots), 0)
        slot_at = lax.broadcasted_iota(jnp.int32, (slots, group_slots), 1)
        wanted = slot_at // (4 * CAP) * (2 * CAP) + zl * CAP + slot_at % CAP
        choose = (slot_in == wanted).astype(BF16)
        row_y = lax.broadcasted_iota(jnp.int32, (4 * rows, group_slots), 0) // rows
        slot_y = lax.broadcasted_iota(jnp.int32, (4 * rows, group_slots), 1) // CAP % 4
        same_y = row_y == slot_y
        s_dx = copies.take(12)

        def select(kz):
            if kz > 0:
                for ky in range(4):
                    copies.arrived(s_dz + 3 * ky + kz - 1, d_raw.at[kz, ky])
            for i in range(2):
                lanes = d_raw[kz, :, :, WIDE + i * slots : WIDE + (i + 1) * slots]
                lanes = jnp.dot(
                    lanes.reshape(4 * rows, slots), choose, preferred_element_type=F32
                )
                d_weights[kz, i] = jnp.where(same_y, lanes, 0.0).astype(BF16)
            chosen = (d_weights[kz, 0].astype(F32) > 0.0).astype(BF16)
            data = d_raw[kz, :, :, 0:WIDE].reshape(4 * rows, WIDE)
            value = lax.dot_general(chosen, data, over_rows, preferred_element_type=F32)
            d_slots[kz] = value.astype(BF16).reshape(4, 4 * CAP, WIDE)
            for i in range(3):
                own.append(
                    copies.send(
                        s_dx + 3 * kz + i, d_slots.at[kz, x_out[i]], d_rows.at[kz, i + 1], x_to[i]
                    )
                )
            d_rows[kz, 0] = d_slots[kz, x]

        def placed(kz):
            for i in range(3):
                copies.arrived(s_dx + 3 * kz + i, d_rows.at[kz, i + 1])
            own.append(share(s_d, d_rows, kz))

        select(0)
        for i in range(3):
            copies.arrived(s_x + i, f_x.at[i + 1])
        split_pairs(f_x, f_z)
        s_up, s_down = copies.take(), copies.take()
        own.append(copies.send(s_up, f_z, f_y.at[0], y_up))
        own.append(copies.send(s_down, f_z, f_y.at[1], y_down))
        s_z = copies.take(12)

        def spread(ky, block, targets):
            for j in targets:
                own.append(
                    copies.send(
                        s_z + 3 * ky + j, block.at[z_out[j] % 2], f_rows.at[j + 1, ky], z_to[j]
                    )
                )

        def gathered(kz):
            for ky in range(4):
                if kz > 0:
                    copies.arrived(s_z + 3 * ky + kz - 1, f_rows.at[kz, ky])
            own.append(share(s_f, f_rows, kz))

        s_bdx, s_bz, s_bdz = copies.take(12), copies.take(3), copies.take(3)

        def project_df(k, count=1):
            inner_wait(k, count)

            def put_d(n, value):
                columns = pl.ds(pl.multiple_of(n * 1024, 1024), 1024)
                for i in range(count):
                    for kx in range(4):
                        for ky in (0, 2):
                            at = i * 128 + ky * 32 + kx * CAP
                            pair = [value[at : at + CAP], value[at + 32 : at + 32 + CAP]]
                            d_part[k + i, kx, ky * CAP : (ky + 2) * CAP, columns] = (
                                jnp.concatenate(pair, axis=0).astype(BF16)
                            )

            def put_f(n, value):
                f_part[k : k + count] = value.astype(BF16).reshape(count, 4, 32, half - WIDE)

            project(k, count, 0, WIDE, put_d)
            for j in range(k, k + count):
                for i in range(3):
                    own.append(
                        copies.send(
                            s_bdx + 3 * j + i,
                            d_part.at[j, i + 1],
                            d_xin.at[j, x],
                            x_to[home[i]],
                        )
                    )
                d_xin[j, x] = d_part[j, 0]
            project(k, count, WIDE, half, put_f)
            for j in range(k, k + count):
                if j > 0:
                    i = j - 1
                    own.append(copies.send(s_bz + i, f_part.at[j], f_zin.at[i], z_to[home[i]]))

        def combine(kz):
            for i, d in enumerate((1, -1, 2)):
                copies.arrived(s_bdx + 3 * kz + i, d_xin.at[kz, shift(x, d)])
            data = d_xin[kz].reshape(group_slots, WIDE)
            value = jnp.dot(d_weights[kz, 0], data, preferred_element_type=F32)
            value += jnp.dot(d_weights[kz, 1], data, preferred_element_type=F32)
            d_group[kz] = value.astype(BF16)
            if kz > 0:
                i = kz - 1
                own.append(copies.send(s_bdz + i, d_group.at[kz], d_zin.at[i], z_to[home[i]]))

        select(1)
        select(2)
        s_up2, s_down2 = copies.take(), copies.take()
        copies.arrived(s_up, f_y.at[0])
        own.append(copies.send(s_up2, f_y.at[0, 0], f_y.at[2, 0], y_up))
        copies.arrived(s_down, f_y.at[1])
        own.append(copies.send(s_down2, f_y.at[1, 1], f_y.at[2, 1], y_down))
        pl.semaphore_wait(turn, 1)
        for ky in range(4):
            raw_to_z(ky, (2,))
        spread(0, f_z, (0, 1))
        spread(1, f_y.at[0], (0, 1))
        spread(2, f_y.at[1], (0, 1))
        f_rows[0, 0] = f_z[z % 2]
        f_rows[0, 1] = f_y[0, z % 2]
        f_rows[0, 2] = f_y[1, z % 2]
        placed(0)
        copies.arrived(s_up2, f_y.at[2, 0])
        copies.arrived(s_down2, f_y.at[2, 1])
        spread(3, f_y.at[2], (0, 1))
        f_rows[0, 3] = f_y[2, z % 2]
        gathered(0)
        for ky, block in enumerate((f_z, f_y.at[0], f_y.at[1], f_y.at[2])):
            spread(ky, block, (2,))
        load_wait()
        add_d(0)
        add_f(0)
        shared(s_e, e_rows, 0)
        add_e(0)
        own.append(activate(0))
        select(3)
        placed(1)
        placed(2)
        gathered(1)
        gathered(2)
        wd_wait()
        project_df(0)
        add_d(1, 2)
        add_f(1, 2)
        placed(3)
        gathered(3)
        shared(s_e, e_rows, 1, 2)
        add_e(1, 2)
        own.append(activate(1, 2))
        combine(0)
        add_d(3)
        project_df(1, 2)
        add_f(3)
        shared(s_e, e_rows, 3)
        add_e(3)
        own.append(activate(3))
        combine(1)
        combine(2)
        project_df(3)
        for i in range(3):
            copies.arrived(s_bz + i, f_zin.at[i])
        s_bup, s_bdown = copies.take(), copies.take()
        s_bup2, s_bdown2 = copies.take(), copies.take()
        for ky in (3, 2, 1, 0):
            f_sum[ky, z % 2] = total_of(f_part[0, ky], f_zin[2, ky])
            f_sum[ky, 1 - z % 2] = total_of(f_zin[0, ky], f_zin[1, ky])
            if ky == 3:
                own.append(copies.send(s_bup, f_sum.at[3, 0], f_up, y_up))
                own.append(copies.send(s_bdown, f_sum.at[3, 1], f_down, y_down))
        combine(3)
        copies.arrived(s_bup, f_up)
        f_sum[2, 0] = total_of(f_sum[2, 0], f_up[...])
        own.append(copies.send(s_bup2, f_sum.at[2], f_up2, y_up))
        copies.arrived(s_bdown, f_down)
        f_sum[1, 1] = total_of(f_sum[1, 1], f_down[...])
        own.append(copies.send(s_bdown2, f_sum.at[1], f_down2, y_down))
        for i in range(3):
            copies.arrived(s_bdz + i, d_zin.at[i])
        value = total_of(d_group[0], d_zin[0], d_zin[1], d_zin[2])
        d_sum[...] = value.reshape(4, rows, WIDE)
        s_dy = copies.take(3)
        for i in range(3):
            own.append(copies.send(s_dy + i, d_sum.at[i + 1], d_yin.at[i], y_to[home[i]]))
        copies.arrived(s_bup2, f_up2)
        copies.arrived(s_bdown2, f_down2)
        f_sum[0] = total_of(f_sum[0], f_up2[...], f_down2[...])
        join_pairs(f_sum.at[0], f_back)
        s_x = copies.take(3)
        own += x_return(s_x, f_back, f_end)
        x_returned(s_x, f_end)
        value = hid[:, WIDE:] + weighted(f_end[...].reshape(slots, half - WIDE))
        last[:, WIDE:] = value.astype(BF16)
        value = hid[:, 0:WIDE] + d_sum[0].astype(F32)
        for i in range(3):
            copies.arrived(s_dy + i, d_yin.at[i])
            value = value + d_yin[i].astype(F32)
        last[:, 0:WIDE] = value.astype(BF16)
        pltpu.make_async_copy(last, o_ref.at[:, mine], load_sems.at[0]).start()
        own.append(copies.send(s_last, last, o_ref.at[:, mine], other))
        for copy in own:
            copy.wait_send()

    common = copies.used
    pl.when(c == 0)(core_zero)
    used_zero, copies.used = copies.used, common
    pl.when(c == 1)(core_one)
    assert max(used_zero, copies.used) <= SEMS

    copies.arrived(s_last, o_ref.at[:, theirs])
    pltpu.make_async_copy(last, o_ref.at[:, mine], load_sems.at[0]).wait()
    for copy in sent:
        copy.wait_send()


def on_device(
    queries,
    new_keys,
    new_values,
    fork_map,
    key_cache,
    value_cache,
    cache_lengths,
    residual,
    norm_gain,
    expert_ids,
    gate_weights,
    w_gate,
    w_up,
    w_down,
):
    rows, width = residual.shape
    half = width // 2
    narrow = half - WIDE
    hidden = w_gate.shape[2]
    prompts, cache_len, kv_width = key_cache.shape
    heads = kv_width // HD
    vmem = pl.BlockSpec(memory_space=VMEM)
    hbm = pl.BlockSpec(memory_space=pl.ANY)
    return pl.pallas_call(
        layer_kernel,
        out_shape=jax.ShapeDtypeStruct((rows, width), BF16),
        in_specs=[pl.BlockSpec(memory_space=pltpu.SMEM)] + [vmem] * 4 + [hbm] * 9,
        out_specs=hbm,
        scratch_shapes=[
            VMEM((rows, half), BF16),
            VMEM((rows, kv_width), BF16),
            VMEM((rows, kv_width), BF16),
            VMEM((heads, prompts, cache_len, HD), BF16),
            VMEM((heads, prompts, cache_len, HD), BF16),
            VMEM((rows, half), BF16),
            VMEM((width, hidden), BF16),
            VMEM((width, hidden), BF16),
            VMEM((2 * hidden, half), BF16),
            VMEM((2, rows, HD), F32),
            VMEM((rows, half), F32),
            VMEM((512, hidden), F32),
            VMEM((512, hidden), F32),
            VMEM((2, 512, hidden), BF16),
            VMEM((rows, half), BF16),
            VMEM((4, 16, half), BF16),
            VMEM((4, 16, half), BF16),
            VMEM((2, 32, half), BF16),
            VMEM((4, 4, 32, half), BF16),
            VMEM((4, 4, 32, half), BF16),
            VMEM((4, 16, half), BF16),
            VMEM((4, 16, half), BF16),
            VMEM((4, 32, half), BF16),
            VMEM((4, 32, half), BF16),
            VMEM((3, 32, half), BF16),
            VMEM((2, 32, half), BF16),
            VMEM((4, 16, half), BF16),
            VMEM((4, 16, half), BF16),
            VMEM((4, 16, narrow), BF16),
            VMEM((4, 16, narrow), BF16),
            VMEM((2, 32, narrow), BF16),
            VMEM((3, 2, 32, narrow), BF16),
            VMEM((4, 4, 32, narrow), BF16),
            VMEM((4, 4, 32, narrow), BF16),
            VMEM((3, 4, 32, narrow), BF16),
            VMEM((4, 2, 32, narrow), BF16),
            VMEM((32, narrow), BF16),
            VMEM((32, narrow), BF16),
            VMEM((2, 32, narrow), BF16),
            VMEM((2, 32, narrow), BF16),
            VMEM((4, 16, narrow), BF16),
            VMEM((4, 16, narrow), BF16),
            VMEM((4, 4, rows, WIDE + HD), BF16),
            VMEM((4, 2, 4 * rows, HD), BF16),
            VMEM((4, 4, 32, WIDE), BF16),
            VMEM((4, 4, 32, WIDE), BF16),
            VMEM((4, 4, 32, WIDE), BF16),
            VMEM((4, 4, 32, WIDE), BF16),
            VMEM((4, 4 * rows, WIDE), BF16),
            VMEM((3, 4 * rows, WIDE), BF16),
            VMEM((4, rows, WIDE), BF16),
            VMEM((3, rows, WIDE), BF16),
            pltpu.SemaphoreType.DMA((SEMS,)),
            pltpu.SemaphoreType.DMA((SEMS,)),
            pltpu.SemaphoreType.DMA((7 + 2 * heads,)),
            pltpu.SemaphoreType.REGULAR,
        ],
        compiler_params=pltpu.CompilerParams(
            collective_id=0, has_side_effects=True, vmem_limit_bytes=60 * 2**20
        ),
    )(
        cache_lengths,
        fork_map.reshape(1, rows),
        norm_gain.reshape(width // HD, HD),
        expert_ids.T,
        gate_weights.T,
        queries,
        new_keys,
        new_values,
        key_cache,
        value_cache,
        residual,
        w_gate[0],
        w_up[0],
        w_down[0],
    )


def solution(mesh):
    in_specs = (
        P(("grp", "shard"), "pool"),
        P(("grp", "shard"), "pool"),
        P(("grp", "shard"), "pool"),
        P(("grp", "shard")),
        P(("grp", "shard"), None, "pool"),
        P(("grp", "shard"), None, "pool"),
        P(("grp", "shard")),
        P(("grp", "shard"), None),
        P(),
        P(("grp", "shard"), None),
        P(("grp", "shard"), None),
        P("grp", None, ("pool", "shard")),
        P("grp", None, ("pool", "shard")),
        P("grp", ("pool", "shard"), None),
    )
    out_specs = P(("grp", "shard"), None)
    return jax.shard_map(
        on_device, mesh=mesh, in_specs=in_specs, out_specs=out_specs, check_vma=False
    )
```

time: 87.5 us -> 80.9 us (0.925)
  Pallas kernels: 85.7 us -> 79.1 us
    pallas_call x1, Pallas kernels: 85.7 us -> 79.1 us  [on_device(): pl.pallas_call(layer_kernel, out_shape=jax.ShapeDtypeStruct((rows, width)...]
where the time goes in v3:
time: 80.9 us; the launch traced here: 80.7 us
  Pallas kernels  79.1 us (98%)
  local copies, waits for them, and re-layouts  1.62 us (2%)
    pallas_call x1, Pallas kernels, on_device(): pl.pallas_call(layer_kernel, out_shape=jax.ShapeDtypeStruct((rows, width)...  79.1 us

profile of v3, /device:TPU:1, one launch (start us, length us, event | category | flops | bytes accessed | tf_op | source)
XLA Modules:
  0.0 80.7 jit_solution(10160806141130661845)
XLA Ops:
  0.0 79.1 %shard_map.136 = bf16[16,6144]{1,0:T(8,128)(2,1)} custom-call(s32[2]{0:T(128)} %lens_ref.1, s32[1,16]{1,0:T(1,128)} %bitcast.13, bf16[48,128]{1,0:T(8,128)(2,1)} %bitcast.10, s32[2,16]{1,0:T(2,128)} %bitcast.11, f32[2,16]{1,0:T(2,128)} %bitcast.12, bf16[16,3072]{1,0:T(8,128)(2,1)} %q_hbm.1, bf16[16,512]{1,0:T(8,128)(2,1)} %nk_hbm.1, bf16[16,512]{1,0:T(8,128)(2,1)} %nv_hbm.1, ...), custom_call_target="tpu_custom_call" | custom-call | tf_op jit(solution)/shard_map/pallas_call | solution.py:831
  79.1 1.6 %copy.16 = bf16[16,6144]{1,0:T(8,128)(2,1)} copy(bf16[16,6144]{1,0:T(8,128)(2,1)} %shard_map.136) | data formatting | bytes 393216

commit v4 on v3

--- a/solution.py
+++ b/solution.py
@@ -166,12 +166,6 @@
             )
         )
     res_load = load(3 + 2 * heads, res_hbm.at[:, mine], res_in)
-    loads = [
-        load(4 + 2 * heads, wg_hbm, wg),
-        load(5 + 2 * heads, wu_hbm, wu),
-        load(6 + 2 * heads, wd_hbm.at[:, mine], wd.at[mine_hidden]),
-    ]
-
     barrier = pltpu.get_barrier_semaphore()
     partners = [other] + x_to + y_to + z_to
     for partner in partners:
@@ -221,6 +215,11 @@
         out = (mixed / total).astype(BF16).astype(F32)
         attended += [out[i * rows : (i + 1) * rows] for i in range(group)]
     attended = jnp.concatenate(attended, axis=1)
+    loads = [
+        load(4 + 2 * heads, wg_hbm, wg),
+        load(5 + 2 * heads, wu_hbm, wu),
+        load(6 + 2 * heads, wd_hbm.at[:, mine], wd.at[mine_hidden]),
+    ]
 
     slots = 4 * rows
     slot = lax.broadcasted_iota(jnp.int32, (slots, rows), 0)
@@ -281,38 +280,50 @@
             dst[2 * pair] = jnp.concatenate([a[:CAP], b[:CAP]], axis=0).astype(BF16)
             dst[2 * pair + 1] = jnp.concatenate([a[CAP:], b[CAP:]], axis=0).astype(BF16)
 
-    def dots(data, weight_rows, put):
+    def dots(parts, put, step):
         for weight, total in ((wg, gate), (wu, up)):
 
-            @pl.loop(0, hidden // 256)
+            @pl.loop(0, hidden // step)
             def _(n):
-                columns = pl.ds(pl.multiple_of(n * 256, 256), 256)
-                value = jnp.dot(data, weight[weight_rows, columns], preferred_element_type=F32)
+                columns = pl.ds(pl.multiple_of(n * step, step), step)
+                value = None
+                for data, weight_rows in parts:
+                    term = jnp.dot(data, weight[weight_rows, columns], preferred_element_type=F32)
+                    value = term if value is None else value + term
                 put(total, columns, value)
 
-    def add_chunk(data, weight_rows, k, count):
+    def e_of(k, count):
+        return e_rows[k : k + count].reshape(count * 128, half), slice(0, half)
+
+    def f_of(k, count):
+        data = f_rows[k : k + count].reshape(count * 128, half - WIDE)
+        return data, slice(half + WIDE, width)
+
+    def add_ef(k, count, use_e, use_f, write):
         at = slice(k * 128, (k + count) * 128)
+        parts = [e_of(k, count)] * use_e + [f_of(k, count)] * use_f
 
         def put(total, columns, value):
-            total[at, columns] += value
-
-        dots(data, weight_rows, put)
-
-    def add_e(k, count=1):
-        add_chunk(e_rows[k : k + count].reshape(count * 128, half), slice(0, half), k, count)
-
-    def add_f(k, count=1):
-        data = f_rows[k : k + count].reshape(count * 128, half - WIDE)
-        add_chunk(data, slice(half + WIDE, width), k, count)
-
-    def add_d(k, count=1):
+            if write:
+                total[at, columns] = value
+            else:
+                total[at, columns] += value
+
+        dots(parts, put, 256)
+
+    def add_d(k, count, write):
         def put(total, columns, value):
             for i in range(count * 16):
                 kz, kx, ky = k + i // 16, i // 4 % 4, i % 4
                 at = kz * 128 + ky * 32 + kx * CAP
-                total[at : at + CAP, columns] += value[i * CAP : (i + 1) * CAP]
-
-        dots(d_rows[k : k + count].reshape(count * 128, WIDE), slice(half, half + WIDE), put)
+                rows_here = value[i * CAP : (i + 1) * CAP]
+                if write:
+                    total[at : at + CAP, columns] = rows_here
+                else:
+                    total[at : at + CAP, columns] += rows_here
+
+        data = d_rows[k : k + count].reshape(count * 128, WIDE)
+        dots([(data, slice(half, half + WIDE))], put, 256)
 
     def share(first, ref, k):
         return copies.send(first + k, ref.at[k], ref.at[k], other)
@@ -333,10 +344,6 @@
     def load_wait():
         for load in loads[:2]:
             load.wait()
-
-    def clear():
-        gate[...] = jnp.zeros_like(gate)
-        up[...] = jnp.zeros_like(up)
 
     def activate(k, count=1):
         at = slice(k * 128, (k + count) * 128)
@@ -399,7 +406,6 @@
         s_x = copies.take(3)
         own += x_send(s_x, e_first, e_x)
         own += share_wd()
-        clear()
         for i in range(3):
             copies.arrived(s_x + i, e_x.at[i + 1])
         split_pairs(e_x, e_z)
@@ -410,7 +416,7 @@
 
         first_z = [to_z(0), to_z(1)]
         e_rows[0, 0] = e_z[z % 2]
-        straight, straight_back = (0, 3), (3,)
+        straight, straight_back = (0, 3), (0, 1, 2, 3)
         s_up, s_down, s_up2, s_down2 = (copies.take(4) for _ in range(4))
 
         def ring(j):
@@ -503,44 +509,40 @@
         ring(1)
         ring(2)
         ringed(0)
-        ring(3)
         load_wait()
-        add_e(0)
+        add_ef(0, 1, True, False, True)
         shared(s_d, d_rows, 0)
-        add_d(0)
-        shared(s_f, f_rows, 0)
-        add_f(0)
-        own.append(activate(0))
+        add_d(0, 1, False)
         forward(1)
         forward(2)
-        wd_wait()
-        project_e(0)
-        forward(3)
+        ring(3)
+        shared(s_f, f_rows, 0)
+        add_ef(0, 1, False, True, False)
+        own.append(activate(0))
+        ringed(1)
         shared(s_d, d_rows, 1, 2)
-        add_d(1, 2)
+        add_d(1, 2, True)
+        ringed(2)
         shared(s_f, f_rows, 1, 2)
-        add_f(1, 2)
-        ringed(1)
-        ringed(2)
-        add_e(1, 2)
+        add_ef(1, 2, True, True, False)
         own.append(activate(1, 2))
-        ring_back(0)
         ringed(3)
         shared(s_d, d_rows, 3)
-        add_d(3)
+        add_d(3, 1, True)
+        wd_wait()
+        project_e(1, 2)
         shared(s_f, f_rows, 3)
-        add_f(3)
-        project_e(1, 2)
-        add_e(3)
+        add_ef(3, 1, True, True, False)
         own.append(activate(3))
         ring_back(1)
         ring_back(2)
         project_e(3)
-        ringed_back(0)
+        project_e(0)
         ringed_back(1)
         ringed_back(2)
-        ring_back(3)
+        ring_back(0)
         ringed_back(3)
+        ringed_back(0)
         for j in range(3):
             copies.arrived(s_bz + j, e_zin.at[j])
         e_sum[z % 2] = total_of(e_part[0, 0], e_zin[2])
@@ -582,7 +584,6 @@
         s_x = copies.take(3)
         own += x_send(s_x, f_first, f_x)
         own += share_wd()
-        clear()
         for ky in (1, 2, 3):
             copies.arrived(s_dy + ky - 1, d_raw.at[0, ky])
             raw_to_z(ky, (0, 1))
@@ -720,35 +721,31 @@
         for ky, block in enumerate((f_z, f_y.at[0], f_y.at[1], f_y.at[2])):
             spread(ky, block, (2,))
         load_wait()
-        add_d(0)
-        add_f(0)
+        add_d(0, 1, True)
         shared(s_e, e_rows, 0)
-        add_e(0)
+        add_ef(0, 1, True, True, False)
         own.append(activate(0))
         select(3)
         placed(1)
         placed(2)
         gathered(1)
         gathered(2)
-        wd_wait()
-        project_df(0)
-        add_d(1, 2)
-        add_f(1, 2)
+        add_d(1, 2, True)
         placed(3)
         gathered(3)
         shared(s_e, e_rows, 1, 2)
-        add_e(1, 2)
+        add_ef(1, 2, True, True, False)
         own.append(activate(1, 2))
-        combine(0)
-        add_d(3)
+        add_d(3, 1, True)
+        wd_wait()
         project_df(1, 2)
-        add_f(3)
         shared(s_e, e_rows, 3)
-        add_e(3)
+        add_ef(3, 1, True, True, False)
         own.append(activate(3))
+        project_df(3)
+        project_df(0)
         combine(1)
         combine(2)
-        project_df(3)
         for i in range(3):
             copies.arrived(s_bz + i, f_zin.at[i])
         s_bup, s_bdown = copies.take(), copies.take()
@@ -760,6 +757,7 @@
                 own.append(copies.send(s_bup, f_sum.at[3, 0], f_up, y_up))
                 own.append(copies.send(s_bdown, f_sum.at[3, 1], f_down, y_down))
         combine(3)
+        combine(0)
         copies.arrived(s_bup, f_up)
         f_sum[2, 0] = total_of(f_sum[2, 0], f_up[...])
         own.append(copies.send(s_bup2, f_sum.at[2], f_up2, y_up))

time: 80.9 us -> 76.4 us (0.944)
  Pallas kernels: 79.1 us -> 74.6 us
    pallas_call x1, Pallas kernels: 79.1 us -> 74.6 us  [on_device(): pl.pallas_call(layer_kernel, out_shape=jax.ShapeDtypeStruct((rows, width)...]
where the time goes in v4:
time: 76.4 us; the launch traced here: 76.3 us
  Pallas kernels  74.6 us (98%)
  local copies, waits for them, and re-layouts  1.62 us (2%)
    pallas_call x1, Pallas kernels, on_device(): pl.pallas_call(layer_kernel, out_shape=jax.ShapeDtypeStruct((rows, width)...  74.6 us
    unnamed x1, local copies, waits for them, and re-layouts  1.62 us

profile of v4, /device:TPU:1, one launch (start us, length us, event | category | flops | bytes accessed | tf_op | source)
XLA Modules:
  0.0 76.3 jit_solution(9403244192230779300)
XLA Ops:
  0.0 74.6 %shard_map.136 = bf16[16,6144]{1,0:T(8,128)(2,1)} custom-call(s32[2]{0:T(128)} %lens_ref.1, s32[1,16]{1,0:T(1,128)} %bitcast.13, bf16[48,128]{1,0:T(8,128)(2,1)} %bitcast.10, s32[2,16]{1,0:T(2,128)} %bitcast.11, f32[2,16]{1,0:T(2,128)} %bitcast.12, bf16[16,3072]{1,0:T(8,128)(2,1)} %q_hbm.1, bf16[16,512]{1,0:T(8,128)(2,1)} %nk_hbm.1, bf16[16,512]{1,0:T(8,128)(2,1)} %nv_hbm.1, ...), custom_call_target="tpu_custom_call" | custom-call | tf_op jit(solution)/shard_map/pallas_call | solution.py:829
  74.6 1.6 %copy.16 = bf16[16,6144]{1,0:T(8,128)(2,1)} copy(bf16[16,6144]{1,0:T(8,128)(2,1)} %shard_map.136) | data formatting | bytes 393216

commit v5 on v4

--- a/solution.py
+++ b/solution.py
@@ -260,6 +260,7 @@
     ).astype(BF16)
     over_rows = (((0,), (0,)), ((), ()))
     s_e, s_f, s_d = copies.take(4), copies.take(4), copies.take(4)
+    s_near = copies.take(4)
     s_inner = copies.take(4)
     s_last = copies.take()
     s_wd = copies.take()
@@ -331,6 +332,11 @@
     def shared(first, ref, k, count=1):
         for i in range(k, k + count):
             copies.arrived(first + i, ref.at[i])
+
+    def shared_e(k, count=1):
+        for i in range(k, k + count):
+            copies.arrived(s_near + i, e_rows.at[i, 0:3])
+            copies.arrived(s_e + i, e_rows.at[i, 3])
 
     def share_wd():
         src = wd_hbm.at[:, theirs]
@@ -427,6 +433,10 @@
             if j in straight:
                 own.append(copies.send(s_up2 + j, e_rows.at[j, 0], e_rows.at[j, 3], y_to[2]))
 
+        def share_near(j):
+            near = e_rows.at[j, 0:3]
+            return copies.send(s_near + j, near, near, other)
+
         def forward(j):
             if j in straight:
                 return
@@ -438,16 +448,19 @@
             own.append(
                 copies.send(s_down2 + j, e_rows.at[j, 2, 16:32], e_rows.at[j, 3, 16:32], y_down)
             )
+            own.append(share_near(j))
 
         def ringed(j):
             if j in straight:
                 copies.arrived(s_up + j, e_rows.at[j, 1])
                 copies.arrived(s_down + j, e_rows.at[j, 2])
+                own.append(share_near(j))
                 copies.arrived(s_up2 + j, e_rows.at[j, 3])
             else:
                 copies.arrived(s_up2 + j, e_rows.at[j, 3, 0:16])
                 copies.arrived(s_down2 + j, e_rows.at[j, 3, 16:32])
-            own.append(share(s_e, e_rows, j))
+            far = e_rows.at[j, 3]
+            own.append(copies.send(s_e + j, far, far, other))
 
         s_bup, s_bdown, s_bup2, s_bdown2 = (copies.take(4) for _ in range(4))
         s_bz = copies.take(3)
@@ -722,7 +735,7 @@
             spread(ky, block, (2,))
         load_wait()
         add_d(0, 1, True)
-        shared(s_e, e_rows, 0)
+        shared_e(0)
         add_ef(0, 1, True, True, False)
         own.append(activate(0))
         select(3)
@@ -733,13 +746,13 @@
         add_d(1, 2, True)
         placed(3)
         gathered(3)
-        shared(s_e, e_rows, 1, 2)
+        shared_e(1, 2)
         add_ef(1, 2, True, True, False)
         own.append(activate(1, 2))
         add_d(3, 1, True)
         wd_wait()
         project_df(1, 2)
-        shared(s_e, e_rows, 3)
+        shared_e(3)
         add_ef(3, 1, True, True, False)
         own.append(activate(3))
         project_df(3)

time: 76.4 us -> 76 us (level)
  no operation moved by 1% of the time
where the time goes in v5:
time: 76 us; the launch traced here: 75.8 us
  Pallas kernels  74.2 us (98%)
  local copies, waits for them, and re-layouts  1.62 us (2%)
    pallas_call x1, Pallas kernels, on_device(): pl.pallas_call(layer_kernel, out_shape=jax.ShapeDtypeStruct((rows, width)...  74.2 us
    unnamed x1, local copies, waits for them, and re-layouts  1.62 us

profile of v5, /device:TPU:1, one launch (start us, length us, event | category | flops | bytes accessed | tf_op | source)
XLA Modules:
  0.0 75.8 jit_solution(13334111041851921791)
XLA Ops:
  0.0 74.2 %shard_map.136 = bf16[16,6144]{1,0:T(8,128)(2,1)} custom-call(s32[2]{0:T(128)} %lens_ref.1, s32[1,16]{1,0:T(1,128)} %bitcast.13, bf16[48,128]{1,0:T(8,128)(2,1)} %bitcast.10, s32[2,16]{1,0:T(2,128)} %bitcast.11, f32[2,16]{1,0:T(2,128)} %bitcast.12, bf16[16,3072]{1,0:T(8,128)(2,1)} %q_hbm.1, bf16[16,512]{1,0:T(8,128)(2,1)} %nk_hbm.1, bf16[16,512]{1,0:T(8,128)(2,1)} %nv_hbm.1, ...), custom_call_target="tpu_custom_call" | custom-call | tf_op jit(solution)/shard_map/pallas_call | solution.py:842
  74.2 1.6 %copy.16 = bf16[16,6144]{1,0:T(8,128)(2,1)} copy(bf16[16,6144]{1,0:T(8,128)(2,1)} %shard_map.136) | data formatting | bytes 393216
